TPU v7x, 512 devices: a whole 4x4x16 slice. The times are simulated.
512 devices in a mesh: ctx: 64 (over z_lo, y, core), tp: 8 (over x, z_hi).
Axes of the slice: x: 4, y: 4, z: 16 (z_hi: 2, z_lo: 8; z = z_hi * 8 + z_lo), core: 2. Of those that a mesh axis runs over, the one named last changes fastest.
Arguments:
- projected: bfloat16 [3, 16384, 2048], P(None, 'ctx', 'tp'), may hold values from -6 to 6
- short_filter: float32 [3, 3, 2048], P(None, None, 'tp'), may hold values from -4 to 4
- decay_rates: float32 [16, 2048], P(None, 'tp'), may hold values from 6.1035156e-05 to 0.05
- residues: float32 [16, 2048], P(None, 'tp'), may hold values from -0.09375 to 0.09375
- output_grad: bfloat16 [16384, 2048], P('ctx', 'tp'), may hold values from -6 to 6
- clip_bound: float32 [1], replicated, may hold values from 2085.3428 to 8688928
Outputs:
- gated_output: bfloat16 [16384, 2048], P('ctx', 'tp')
- projected_grads: bfloat16 [3, 16384, 2048], P(None, 'ctx', 'tp')
- filter_grads: float32 [3, 3, 2048], P(None, None, 'tp')
All inputs are finite; a program needn't handle non-finite values.
Results may differ from a plain program's by a relative error of at most 0.0082.
Values may be sent and summed in bfloat16 or wider, within the bound.
A program may use at most 64 MiB of HBM per device.

v0:
```python
import math

import jax
import jax.numpy as jnp
from jax import lax
from jax.sharding import PartitionSpec as P

FB = 512


def shifted(value, axis, steps):
    count = lax.axis_size(axis)
    leading, last = (max(0, -steps), min(count, count - steps))
    return lax.ppermute(value, axis, [(source, source + steps) for source in range(leading, last)])


def trig_table(rows, cols, modulus):
    index = (
        jnp.arange(rows, dtype=jnp.int32)[:, None]
        * jnp.arange(cols, dtype=jnp.int32)[None, :]
        % modulus
    )
    angle = index.astype(jnp.float32) * (2.0 * math.pi / modulus)
    return (jnp.cos(angle), jnp.sin(angle))


def filter_spectrum(rates, weights, freq_rows, cols):
    total = freq_rows * cols
    low = jnp.arange(freq_rows, dtype=jnp.int32)[:, None]
    high = jnp.arange(cols, dtype=jnp.int32)[None, :]
    index = low + freq_rows * high
    half_angle = index.astype(jnp.float32) * (math.pi / total)
    sine_half = jnp.sin(half_angle)[None, :, :]
    sine_full = jnp.sin(2.0 * half_angle)[None, :, :]
    parity = (1 - 2 * (index % 2)).astype(jnp.float32)[None, :, :]
    bend = 2.0 * sine_half * sine_half
    resp_real = jnp.zeros((rates.shape[1], freq_rows, cols), jnp.float32)
    resp_imag = jnp.zeros((rates.shape[1], freq_rows, cols), jnp.float32)
    for mode in range(rates.shape[0]):
        rate = rates[mode][:, None, None]
        keep = jnp.exp(-rate)
        gap = -jnp.expm1(-rate)
        tail = jnp.exp(-rate * (total // 2))
        numer = weights[mode][:, None, None] * (1.0 - tail * parity)
        denom = gap * gap + 2.0 * keep * bend
        resp_real = resp_real + numer * (gap + keep * bend) / denom
        resp_imag = resp_imag - numer * keep * sine_full / denom
    return (resp_real, resp_imag)


def filter_pass(real_in, imag_in, resp_real, resp_imag):
    channels, rows, cols = real_in.shape
    freq_rows = 2 * rows
    total = freq_rows * cols
    cos_a, sin_a = trig_table(freq_rows, rows, freq_rows)
    table_a = jnp.concatenate([cos_a, sin_a], axis=0).astype(jnp.bfloat16)
    from_real = jnp.einsum("ka,cab->ckb", table_a, real_in, preferred_element_type=jnp.float32)
    from_imag = jnp.einsum("ka,cab->ckb", table_a, imag_in, preferred_element_type=jnp.float32)
    first_real = from_real[:, :freq_rows] + from_imag[:, freq_rows:]
    first_imag = from_imag[:, :freq_rows] - from_real[:, freq_rows:]
    cos_t, sin_t = trig_table(freq_rows, cols, total)
    cos_t = cos_t[None, :, :]
    sin_t = sin_t[None, :, :]
    twist_real = (first_real * cos_t + first_imag * sin_t).astype(jnp.bfloat16)
    twist_imag = (first_imag * cos_t - first_real * sin_t).astype(jnp.bfloat16)
    cos_b, sin_b = trig_table(cols, cols, cols)
    table_b = jnp.concatenate([cos_b, sin_b], axis=1).astype(jnp.bfloat16)
    second_real = jnp.einsum("ckb,bm->ckm", twist_real, table_b, preferred_element_type=jnp.float32)
    second_imag = jnp.einsum("ckb,bm->ckm", twist_imag, table_b, preferred_element_type=jnp.float32)
    spec_real = second_real[:, :, :cols] + second_imag[:, :, cols:]
    spec_imag = second_imag[:, :, :cols] - second_real[:, :, cols:]
    scale = 1.0 / total
    prod_real = ((resp_real * spec_real - resp_imag * spec_imag) * scale).astype(jnp.bfloat16)
    prod_imag = ((resp_real * spec_imag + resp_imag * spec_real) * scale).astype(jnp.bfloat16)
    back_real = jnp.einsum("ckm,mb->ckb", prod_real, table_b, preferred_element_type=jnp.float32)
    back_imag = jnp.einsum("ckm,mb->ckb", prod_imag, table_b, preferred_element_type=jnp.float32)
    third_real = back_real[:, :, :cols] - back_imag[:, :, cols:]
    third_imag = back_imag[:, :, :cols] + back_real[:, :, cols:]
    turn_real = (third_real * cos_t - third_imag * sin_t).astype(jnp.bfloat16)
    turn_imag = (third_imag * cos_t + third_real * sin_t).astype(jnp.bfloat16)
    cos_c, sin_c = trig_table(rows, freq_rows, freq_rows)
    table_c = jnp.concatenate([cos_c, sin_c], axis=0).astype(jnp.bfloat16)
    last_real = jnp.einsum("ak,ckb->cab", table_c, turn_real, preferred_element_type=jnp.float32)
    last_imag = jnp.einsum("ak,ckb->cab", table_c, turn_imag, preferred_element_type=jnp.float32)
    out_real = last_real[:, :rows] - last_imag[:, rows:]
    out_imag = last_imag[:, :rows] + last_real[:, rows:]
    return (out_real.reshape(channels, rows * cols), out_imag.reshape(channels, rows * cols))


def local(projected, short_filter, decay_rates, residues, output_grad, clip_bound):
    taps = short_filter.shape[1]
    tokens = projected.shape[1]
    lead = taps - 1
    leading = shifted(projected[:, tokens - lead :, :], "ctx", 1)
    extended = jnp.concatenate([leading, projected], axis=1).astype(jnp.float32)
    features = jnp.zeros((3, tokens, projected.shape[2]), jnp.float32)
    for j in range(taps):
        features = (
            features + short_filter[:, j][:, None, :] * extended[:, lead - j : lead - j + tokens]
        )
    cotangent = output_grad.astype(jnp.float32)
    mixer_input = (features[1] * features[2]).astype(jnp.bfloat16)
    grad_input = (cotangent * features[0]).astype(jnp.bfloat16)
    sliver_mix, sliver_grad = (
        lax.all_to_all(jnp.transpose(mixer_input), "ctx", split_axis=0, concat_axis=1, tiled=True),
        lax.all_to_all(jnp.transpose(grad_input), "ctx", split_axis=0, concat_axis=1, tiled=True),
    )
    channels, seq_len = sliver_mix.shape
    rows = seq_len // FB
    start = lax.axis_index("ctx") * channels
    rates = lax.dynamic_slice_in_dim(decay_rates, start, channels, 1)
    modes = lax.dynamic_slice_in_dim(residues, start, channels, 1)
    resp_real, resp_imag = filter_spectrum(rates, modes, 2 * rows, FB)
    real_in = sliver_mix.reshape(channels, rows, FB)
    imag_in = jnp.flip(sliver_grad, 1).reshape(channels, rows, FB)
    out_real, out_imag = filter_pass(real_in, imag_in, resp_real, resp_imag)
    sliver_out = out_real.astype(jnp.bfloat16)
    sliver_back = jnp.flip(out_imag, 1).astype(jnp.bfloat16)
    conv_output, conv_grad = (
        lax.all_to_all(sliver_out, "ctx", split_axis=1, concat_axis=0, tiled=True),
        lax.all_to_all(sliver_back, "ctx", split_axis=1, concat_axis=0, tiled=True),
    )
    conv_output = jnp.transpose(conv_output).astype(jnp.float32)
    conv_grad = jnp.transpose(conv_grad).astype(jnp.float32)
    gated_output = (features[0] * conv_output).astype(jnp.bfloat16)
    feature_grads = jnp.stack(
        [cotangent * conv_output, conv_grad * features[2], conv_grad * features[1]]
    )
    trailing = shifted(feature_grads[:, :lead, :], "ctx", -1)
    extended_grads = jnp.concatenate([feature_grads, trailing], axis=1)
    back = jnp.zeros_like(feature_grads)
    sums = []
    for j in range(taps):
        back = back + short_filter[:, j][:, None, :] * extended_grads[:, j : j + tokens]
        sums.append(jnp.sum(feature_grads * extended[:, lead - j : lead - j + tokens], axis=1))
    projected_grads = back.astype(jnp.bfloat16)
    filter_sums = lax.psum(jnp.stack(sums, axis=1), "ctx")
    squared = lax.psum(jnp.sum(filter_sums * filter_sums), "tp")
    grad_norm = jnp.sqrt(squared)
    bound = clip_bound[0]
    filter_grads = filter_sums * (bound / jnp.maximum(grad_norm, bound))
    return (gated_output, projected_grads, filter_grads)


def solution(mesh):
    placed = (
        P(None, "ctx", "tp"),
        P(None, None, "tp"),
        P(None, "tp"),
        P(None, "tp"),
        P("ctx", "tp"),
        P(),
    )
    return jax.shard_map(
        local,
        mesh=mesh,
        in_specs=placed,
        out_specs=(P("ctx", "tp"), P(None, "ctx", "tp"), P(None, None, "tp")),
        check_vma=False,
    )
```

profile of v0, /device:TPU:1, one launch (start us, length us, event | category | flops | bytes accessed | tf_op | source)
XLA Modules:
  0.0 675.9 jit_solution(14274491404004814057)
XLA Ops:
  0.6 0.8 slice.193
  1.6 4.6 collective-permute-start
  6.2 1.2 negate_bitcast_fusion.15
  7.5 0.6 exponential_bitcast_fusion.5
  8.1 0.6 exponential_bitcast_fusion.9
  8.7 0.6 exponential_bitcast_fusion.13
  9.4 0.6 exponential_bitcast_fusion.17
  10.0 0.6 exponential_bitcast_fusion.21
  10.7 0.6 exponential_bitcast_fusion.25
  11.3 0.6 exponential_bitcast_fusion.29
  11.9 1.5 multiply_multiply_fusion
  13.5 0.8 fusion.67
  14.4 1.1 dynamic-slice_bitcast_fusion.15
  15.7 1.2 copy.13
  17.4 0.8 multiply_add_fusion
  18.3 0.7 all_to_all.44
  19.0 15.5 %all-to-all-start = ((bf16[64,4,256]{2,1,0:T(4,128)(2,1)}), bf16[64,4,256]{2,1,0:T(4,128)(2,1)S(1)}, u32[]{:S(2)}, u32[]{:S(2)}) async-start(bf16[64,4,256]{2,1,0:T(4,128)(2,1)} %all_to_all.44), calls=%async_computation | async-start | bytes 262144 | tf_op jit(solution)/shard_map/all_to_all | solution.py:105
  34.9 4.9 divide_add_fusion
  39.8 0.7 all_to_all.47
  40.5 8.7 %all-to-all-done = bf16[64,4,256]{2,1,0:T(4,128)(2,1)S(1)} async-done(((bf16[64,4,256]{2,1,0:T(4,128)(2,1)}), bf16[64,4,256]{2,1,0:T(4,128)(2,1)S(1)}, u32[]{:S(2)}, u32[]{:S(2)}) %all-to-all-start) | async-done | bytes 131104 | tf_op jit(solution)/shard_map/all_to_all | solution.py:105
  49.2 6.0 all-to-all-start.1
  55.2 4.9 divide_subtract_fusion
  60.0 0.7 sine_convert_fusion.2
  60.8 1.2 fusion.47
  62.1 5.2 sine_convert_fusion
  67.2 0.7 copy.14
  67.9 1.6 reshape.827
  69.7 56.5 %rev.8 = bf16[4,16384]{1,0:T(4,128)(2,1)} reverse(bf16[4,16384]{1,0:T(4,128)(2,1)} %bitcast.89), dimensions={1} | reverse | bytes 262144 | tf_op jit(solution)/shard_map/jit(_flip)/rev | solution.py:115
  126.2 1.4 convolution_bitcast_fusion.1
  127.7 0.4 convolution_bitcast_fusion
  128.1 0.5 fusion.11
  128.7 0.5 fusion.12
  129.2 0.6 fusion.13
  129.7 0.6 fusion.14
  131.0 0.8 copy.16
  131.8 13.0 %all-to-all-start.2 = ((bf16[4,64,256]{2,0,1:T(4,128)(2,1)}), bf16[4,64,256]{2,0,1:T(4,128)(2,1)S(1)}, u32[]{:S(2)}, u32[]{:S(2)}) async-start(bf16[4,64,256]{2,0,1:T(4,128)(2,1)} %copy.16), calls=%async_computation.2 | async-start | bytes 262144 | tf_op jit(solution)/shard_map/all_to_all | solution.py:120
  145.0 41.3 %rev.9 = bf16[4,16384]{1,0:T(4,128)(2,1)} reverse(bf16[4,16384]{1,0:T(4,128)(2,1)S(1)} %bitcast.292), dimensions={1} | reverse | bytes 262144 | tf_op jit(solution)/shard_map/jit(_flip)/rev | solution.py:118
  186.3 13.2 %all-to-all-start.3 = ((bf16[4,64,256]{2,0,1:T(4,128)(2,1)}), bf16[4,64,256]{2,0,1:T(4,128)(2,1)S(1)}, u32[]{:S(2)}, u32[]{:S(2)}) async-start(bf16[4,64,256]{2,0,1:T(4,128)(2,1)} %bitcast.98), calls=%async_computation.3 | async-start | bytes 262144 | tf_op jit(solution)/shard_map/all_to_all | solution.py:121
  199.6 14.5 %all-to-all-done.3 = bf16[4,64,256]{2,0,1:T(4,128)(2,1)S(1)} async-done(((bf16[4,64,256]{2,0,1:T(4,128)(2,1)}), bf16[4,64,256]{2,0,1:T(4,128)(2,1)S(1)}, u32[]{:S(2)}, u32[]{:S(2)}) %all-to-all-start.3) | async-done | bytes 131104 | tf_op jit(solution)/shard_map/all_to_all | solution.py:121
  214.4 2.3 collective-permute-start.1
  217.4 6.1 collective-permute-done.1
  223.6 1.5 multiply_reduce_fusion.2
  225.2 408.2 %psum.14 = f32[3,3,256]{2,0,1:T(4,128)S(1)} all-reduce(f32[3,3,256]{2,0,1:T(4,128)S(1)} %pad_maximum_fusion.2), channel_id=1, replica_groups=mesh['ctx'=64,'tp'=8] {'ctx'}, use_global_device_ids=true, to_apply=%region_3.4 | all-reduce | flops 2304 | bytes 18432 | tf_op jit(solution)/shard_map/psum | solution.py:137
  633.4 0.6 multiply_reduce_fusion.3
  634.0 0.8 copy.17
  634.8 38.9 %psum.15 = f32[]{:T(128)} all-reduce(f32[]{:T(128)} %multiply_reduce_fusion.3), channel_id=1, replica_groups=mesh['ctx'=64,'tp'=8] {'tp'}, use_global_device_ids=true, to_apply=%region_5.6 | all-reduce | flops 1 | bytes 8 | tf_op jit(solution)/shard_map/psum | solution.py:138
  674.4 0.6 copy.19
  675.0 0.9 copy.18
  (141 shorter events, 2.7 us)
Async XLA Ops:
  0.6 16.2 %copy-start.8 = (bf16[256,256]{1,0:T(8,128)(2,1)S(1)}, bf16[256,256]{1,0:T(8,128)(2,1)}, u32[]{:S(2)}) copy-start(bf16[256,256]{1,0:T(8,128)(2,1)} %param.10) | copy-start | bytes 393220
  1.6 15.4 %collective-permute-start = (bf16[3,2,256]{1,2,0:T(8,128)(2,1)S(1)}, bf16[3,2,256]{1,2,0:T(8,128)(2,1)S(1)}, u32[]{:S(2)}, u32[]{:S(2)}) collective-permute-start(bf16[3,2,256]{1,2,0:T(8,128)(2,1)S(1)} %copy.12), channel_id=1, source_target_pairs={{0,8},{8,16},{16,24},{24,32},{32,40},{40,48},{48,56},{56,64},{64,7... | collective-permute-start | bytes 9224 | tf_op jit(solution)/shard_map/ppermute | solution.py:14
  7.4 27.1 %copy-start.45 = (f32[4]{0:T(128)}, f32[4]{0:T(128)S(1)}, u32[]{:S(2)}) copy-start(f32[4]{0:T(128)S(1)} %get-tuple-element.144) | copy-start | bytes 52
  7.4 27.1 %copy-start.46 = (f32[4]{0:T(128)}, f32[4]{0:T(128)S(1)}, u32[]{:S(2)}) copy-start(f32[4]{0:T(128)S(1)} %get-tuple-element.145) | copy-start | bytes 52
  7.4 27.1 %copy-start.47 = (f32[4]{0:T(128)}, f32[4]{0:T(128)S(1)}, u32[]{:S(2)}) copy-start(f32[4]{0:T(128)S(1)} %get-tuple-element.146) | copy-start | bytes 52
  7.5 27.1 %copy-start.48 = (f32[4]{0:T(128)}, f32[4]{0:T(128)S(1)}, u32[]{:S(2)}) copy-start(f32[4]{0:T(128)S(1)} %get-tuple-element.147) | copy-start | bytes 52
  7.5 27.1 %copy-start.49 = (f32[4]{0:T(128)}, f32[4]{0:T(128)S(1)}, u32[]{:S(2)}) copy-start(f32[4]{0:T(128)S(1)} %get-tuple-element.148) | copy-start | bytes 52
  7.5 27.1 %copy-start.50 = (f32[4]{0:T(128)}, f32[4]{0:T(128)S(1)}, u32[]{:S(2)}) copy-start(f32[4]{0:T(128)S(1)} %get-tuple-element.149) | copy-start | bytes 52
  7.5 27.1 %copy-start.29 = (f32[4]{0:T(128)}, f32[4]{0:T(128)S(1)}, u32[]{:S(2)}) copy-start(f32[4]{0:T(128)S(1)} %get-tuple-element.171) | copy-start | bytes 52
  7.5 27.1 %copy-start.30 = (f32[4]{0:T(128)}, f32[4]{0:T(128)S(1)}, u32[]{:S(2)}) copy-start(f32[4]{0:T(128)S(1)} %get-tuple-element.172) | copy-start | bytes 52
  8.1 26.5 %copy-start.51 = (f32[4]{0:T(128)}, f32[4]{0:T(128)S(1)}, u32[]{:S(2)}) copy-start(f32[4]{0:T(128)S(1)} %get-tuple-element.138) | copy-start | bytes 52
  8.1 26.5 %copy-start.31 = (f32[4]{0:T(128)}, f32[4]{0:T(128)S(1)}, u32[]{:S(2)}) copy-start(f32[4]{0:T(128)S(1)} %get-tuple-element.173) | copy-start | bytes 52
  8.1 26.5 %copy-start.32 = (f32[4]{0:T(128)}, f32[4]{0:T(128)S(1)}, u32[]{:S(2)}) copy-start(f32[4]{0:T(128)S(1)} %get-tuple-element.174) | copy-start | bytes 52
  8.7 25.9 %copy-start.33 = (f32[4]{0:T(128)}, f32[4]{0:T(128)S(1)}, u32[]{:S(2)}) copy-start(f32[4]{0:T(128)S(1)} %get-tuple-element.175) | copy-start | bytes 52
  8.7 25.9 %copy-start.34 = (f32[4]{0:T(128)}, f32[4]{0:T(128)S(1)}, u32[]{:S(2)}) copy-start(f32[4]{0:T(128)S(1)} %get-tuple-element.176) | copy-start | bytes 52
  9.4 25.3 %copy-start.35 = (f32[4]{0:T(128)}, f32[4]{0:T(128)S(1)}, u32[]{:S(2)}) copy-start(f32[4]{0:T(128)S(1)} %get-tuple-element.177) | copy-start | bytes 52
  9.4 25.3 %copy-start.36 = (f32[4]{0:T(128)}, f32[4]{0:T(128)S(1)}, u32[]{:S(2)}) copy-start(f32[4]{0:T(128)S(1)} %get-tuple-element.178) | copy-start | bytes 52
  10.0 24.7 %copy-start.37 = (f32[4]{0:T(128)}, f32[4]{0:T(128)S(1)}, u32[]{:S(2)}) copy-start(f32[4]{0:T(128)S(1)} %get-tuple-element.179) | copy-start | bytes 52
  10.0 24.7 %copy-start.38 = (f32[4]{0:T(128)}, f32[4]{0:T(128)S(1)}, u32[]{:S(2)}) copy-start(f32[4]{0:T(128)S(1)} %get-tuple-element.180) | copy-start | bytes 52
  10.6 24.1 %copy-start.39 = (f32[4]{0:T(128)}, f32[4]{0:T(128)S(1)}, u32[]{:S(2)}) copy-start(f32[4]{0:T(128)S(1)} %get-tuple-element.181) | copy-start | bytes 52
  10.6 24.1 %copy-start.40 = (f32[4]{0:T(128)}, f32[4]{0:T(128)S(1)}, u32[]{:S(2)}) copy-start(f32[4]{0:T(128)S(1)} %get-tuple-element.182) | copy-start | bytes 52
  11.3 23.5 %copy-start.41 = (f32[4]{0:T(128)}, f32[4]{0:T(128)S(1)}, u32[]{:S(2)}) copy-start(f32[4]{0:T(128)S(1)} %get-tuple-element.183) | copy-start | bytes 52
  11.3 23.5 %copy-start.42 = (f32[4]{0:T(128)}, f32[4]{0:T(128)S(1)}, u32[]{:S(2)}) copy-start(f32[4]{0:T(128)S(1)} %get-tuple-element.184) | copy-start | bytes 52
  11.9 22.8 %copy-start.43 = (f32[4]{0:T(128)}, f32[4]{0:T(128)S(1)}, u32[]{:S(2)}) copy-start(f32[4]{0:T(128)S(1)} %get-tuple-element.185) | copy-start | bytes 52
  11.9 22.8 %copy-start.44 = (f32[4]{0:T(128)}, f32[4]{0:T(128)S(1)}, u32[]{:S(2)}) copy-start(f32[4]{0:T(128)S(1)} %get-tuple-element.186) | copy-start | bytes 52
  15.6 19.2 %copy-start.17 = (f32[4]{0:T(128)}, f32[4]{0:T(128)S(1)}, u32[]{:S(2)}) copy-start(f32[4]{0:T(128)S(1)} %get-tuple-element.52) | copy-start | bytes 52
  15.6 19.2 %copy-start.18 = (f32[4]{0:T(128)}, f32[4]{0:T(128)S(1)}, u32[]{:S(2)}) copy-start(f32[4]{0:T(128)S(1)} %get-tuple-element.53) | copy-start | bytes 52
  15.6 19.2 %copy-start.19 = (f32[4]{0:T(128)}, f32[4]{0:T(128)S(1)}, u32[]{:S(2)}) copy-start(f32[4]{0:T(128)S(1)} %get-tuple-element.54) | copy-start | bytes 52
  15.6 19.2 %copy-start.20 = (f32[4]{0:T(128)}, f32[4]{0:T(128)S(1)}, u32[]{:S(2)}) copy-start(f32[4]{0:T(128)S(1)} %get-tuple-element.55) | copy-start | bytes 52
  15.6 19.2 %copy-start.21 = (f32[4]{0:T(128)}, f32[4]{0:T(128)S(1)}, u32[]{:S(2)}) copy-start(f32[4]{0:T(128)S(1)} %get-tuple-element.56) | copy-start | bytes 52
  15.6 19.2 %copy-start.22 = (f32[4]{0:T(128)}, f32[4]{0:T(128)S(1)}, u32[]{:S(2)}) copy-start(f32[4]{0:T(128)S(1)} %get-tuple-element.57) | copy-start | bytes 52
  15.6 19.2 %copy-start.23 = (f32[4]{0:T(128)}, f32[4]{0:T(128)S(1)}, u32[]{:S(2)}) copy-start(f32[4]{0:T(128)S(1)} %get-tuple-element.58) | copy-start | bytes 52
  15.6 19.2 %copy-start.24 = (f32[4]{0:T(128)}, f32[4]{0:T(128)S(1)}, u32[]{:S(2)}) copy-start(f32[4]{0:T(128)S(1)} %get-tuple-element.59) | copy-start | bytes 52
  15.6 19.2 %copy-start.25 = (f32[4]{0:T(128)}, f32[4]{0:T(128)S(1)}, u32[]{:S(2)}) copy-start(f32[4]{0:T(128)S(1)} %get-tuple-element.60) | copy-start | bytes 52
  15.6 19.2 %copy-start.26 = (f32[4]{0:T(128)}, f32[4]{0:T(128)S(1)}, u32[]{:S(2)}) copy-start(f32[4]{0:T(128)S(1)} %get-tuple-element.61) | copy-start | bytes 52
  15.7 19.2 %copy-start.27 = (f32[4]{0:T(128)}, f32[4]{0:T(128)S(1)}, u32[]{:S(2)}) copy-start(f32[4]{0:T(128)S(1)} %get-tuple-element.62) | copy-start | bytes 52
  15.7 19.2 %copy-start.28 = (f32[4]{0:T(128)}, f32[4]{0:T(128)S(1)}, u32[]{:S(2)}) copy-start(f32[4]{0:T(128)S(1)} %get-tuple-element.63) | copy-start | bytes 52
  19.0 30.2 %all-to-all-start = ((bf16[64,4,256]{2,1,0:T(4,128)(2,1)}), bf16[64,4,256]{2,1,0:T(4,128)(2,1)S(1)}, u32[]{:S(2)}, u32[]{:S(2)}) async-start(bf16[64,4,256]{2,1,0:T(4,128)(2,1)} %all_to_all.44), calls=%async_computation | async-start | bytes 262144 | tf_op jit(solution)/shard_map/all_to_all | solution.py:105
  49.2 6.0 copy-start.6
  49.2 20.5 %all-to-all-start.1 = ((bf16[64,4,256]{2,1,0:T(4,128)(2,1)}), bf16[64,4,256]{2,1,0:T(4,128)(2,1)}, u32[]{:S(2)}, u32[]{:S(2)}) async-start(bf16[64,4,256]{2,1,0:T(4,128)(2,1)} %all_to_all.47), calls=%async_computation.1 | async-start | bytes 262144 | tf_op jit(solution)/shard_map/all_to_all | solution.py:106
  55.2 12.1 %copy-start.7 = (bf16[64,4,256]{2,1,0:T(4,128)(2,1)S(1)}, bf16[64,4,256]{2,1,0:T(4,128)(2,1)}, u32[]{:S(2)}) copy-start(bf16[64,4,256]{2,1,0:T(4,128)(2,1)} %copy-done.6) | copy-start | bytes 393220
  131.8 54.5 %all-to-all-start.2 = ((bf16[4,64,256]{2,0,1:T(4,128)(2,1)}), bf16[4,64,256]{2,0,1:T(4,128)(2,1)S(1)}, u32[]{:S(2)}, u32[]{:S(2)}) async-start(bf16[4,64,256]{2,0,1:T(4,128)(2,1)} %copy.16), calls=%async_computation.2 | async-start | bytes 262144 | tf_op jit(solution)/shard_map/all_to_all | solution.py:120
  145.0 69.2 %copy-start.4 = (bf16[256,256]{0,1:T(8,128)(2,1)S(1)}, bf16[256,256]{0,1:T(8,128)(2,1)}, u32[]{:S(2)}) copy-start(bf16[256,256]{0,1:T(8,128)(2,1)} %copy-done.3) | copy-start | bytes 393220
  186.3 27.8 %all-to-all-start.3 = ((bf16[4,64,256]{2,0,1:T(4,128)(2,1)}), bf16[4,64,256]{2,0,1:T(4,128)(2,1)S(1)}, u32[]{:S(2)}, u32[]{:S(2)}) async-start(bf16[4,64,256]{2,0,1:T(4,128)(2,1)} %bitcast.98), calls=%async_computation.3 | async-start | bytes 262144 | tf_op jit(solution)/shard_map/all_to_all | solution.py:121
  214.4 9.1 %collective-permute-start.1 = (f32[3,2,256]{1,2,0:T(8,128)S(1)}, f32[3,2,256]{1,2,0:T(8,128)S(1)}, u32[]{:S(2)}, u32[]{:S(2)}) collective-permute-start(f32[3,2,256]{1,2,0:T(8,128)S(1)} %slice.275), channel_id=1, source_target_pairs={{8,0},{16,8},{24,16},{32,24},{40,32},{48,40},{56,48},{64,56},{72,6... | collective-permute-start | bytes 18440 | tf_op jit(solution)/shard_map/ppermute | solution.py:14
  217.4 6.2 copy-start.12
  217.4 6.2 copy-start.14
  217.4 6.2 copy-start.16
  (10 other events, 17.7 us)
where the time goes:
time: 689 us; the launch traced here: 676 us
  blocking collectives  447 us (65%)
  local copies, waits for them, and re-layouts  109 us (16%)
  starting transfers between devices  54.5 us (8%)
  waiting for transfers between devices  29.5 us (4%)
  other arithmetic  27.7 us (4%)
    psum x1, blocking collectives, local(): filter_sums = lax.psum(jnp.stack(sums, axis=1), 'ctx')  408 us
    rev x1, local copies, waits for them, and re-layouts, local(): imag_in = jnp.flip(sliver_grad, 1).reshape(channels, rows, FB)  56.5 us
    rev x1, local copies, waits for them, and re-layouts, local(): sliver_back = jnp.flip(out_imag, 1).astype(jnp.bfloat16)  41.3 us
    psum x1, blocking collectives, local(): squared = lax.psum(jnp.sum(filter_sums * filter_sums), 'tp')  38.9 us
    all_to_all x1, starting transfers between devices, local(): lax.all_to_all(jnp.transpose(mixer_input), 'ctx', split_axis=0, concat_ax...  15.5 us
    all_to_all x1, waiting for transfers between devices, local(): lax.all_to_all(sliver_back, 'ctx', split_axis=1, concat_axis=0, tiled=True)  14.5 us
  transfers between devices with their start and end apart: 6, of which 4 were waited for; matrix products, arithmetic and copies ran while one was open for 11% of the time, Pallas kernels for 0%

commit v1 on v0

v1 whole, which is shorter than its diff:
```python
import functools

import jax
import jax.numpy as jnp
from jax import lax
from jax.experimental import pallas as pl
from jax.experimental.pallas import tpu as pltpu
from jax.sharding import PartitionSpec as P

MESH = pl.DeviceIdType.MESH
F32 = jnp.float32
LANES = 128
SUB = 8
PAD = 8
G = 8
HALO, S_GROUP, S_LINE, S_BACK, R_GROUP, R_LINE, R_BACK, NORM, TAIL = range(9)


def kernel(
    modes, tp_size,
    proj, taps, rates, weights, cot, bound,
    gated, grads, filt,
    pf, feat, xs, ys, lam, htab, excl, rown, gat, fgs,
    halo_out, halo_in, tail_out, tail_in,
    sa_out, sa_in, sb_out, sb_in, sc_out, sc_in,
    r1_out, r1_in, r2_out, r2_in, r3_out, r3_in, r4_out, r4_in,
    ssem, rsem,
):
    tokens = proj.shape[1]
    halves = proj.shape[2] // LANES
    block = tokens // SUB
    quarter = modes // (G // 2)
    ctx, tp = lax.axis_index("ctx"), lax.axis_index("tp")
    count = lax.axis_size("ctx")
    lines = count // G
    z, g = ctx // G, lax.rem(ctx, G)
    causal = g < G // 2
    zz = jnp.where(causal, z, lines - 1 - z)
    towards = jnp.where(causal, 1, -1)

    def at_group(d):
        return {"ctx": z * G + lax.rem(g + d, G), "tp": tp}

    def at_line(d):
        return {"ctx": lax.rem(z + d, lines) * G + g, "tp": tp}

    def at_tp(d):
        return {"ctx": ctx, "tp": lax.rem(tp + d, tp_size)}

    def at(c):
        return {"ctx": c, "tp": tp}

    halo_in[...] = jnp.zeros_like(halo_in)
    tail_in[...] = jnp.zeros_like(tail_in)
    sb_in[...] = jnp.zeros_like(sb_in)

    barrier = pltpu.get_barrier_semaphore()
    for d in range(1, G):
        pl.semaphore_signal(barrier, inc=1, device_id=at_group(d), device_id_type=MESH)
    for d in range(1, lines):
        pl.semaphore_signal(barrier, inc=1, device_id=at_line(d), device_id_type=MESH)
    for d in range(1, tp_size):
        pl.semaphore_signal(barrier, inc=1, device_id=at_tp(d), device_id_type=MESH)
    more_next = jnp.logical_and(g == G - 1, ctx < count - 1)
    more_prev = jnp.logical_and(g == 0, ctx > 0)

    @pl.when(more_next)
    def _():
        pl.semaphore_signal(barrier, inc=1, device_id=at(ctx + 1), device_id_type=MESH)

    @pl.when(more_prev)
    def _():
        pl.semaphore_signal(barrier, inc=1, device_id=at(ctx - 1), device_id_type=MESH)

    def send(src, dst, step, d, dev):
        return pltpu.make_async_remote_copy(
            src_ref=src, dst_ref=dst, send_sem=ssem.at[step, d], recv_sem=rsem.at[step, d],
            device_id=dev, device_id_type=MESH,
        )

    halo_out[...] = jnp.zeros_like(halo_out)
    tail_out[...] = jnp.zeros_like(tail_out)
    r1_out[...] = jnp.zeros_like(r1_out)
    for s in range(3):
        last = proj[s, tokens - 16 : tokens, :].astype(F32)
        halo_out[2 * s : 2 * s + 2, :] = last[14:16, :]

    pl.semaphore_wait(
        barrier,
        (G - 1) + (lines - 1) + (tp_size - 1) + jnp.where(more_next, 1, 0) + jnp.where(more_prev, 1, 0),
    )
    halo = send(halo_out, halo_in, HALO, 0, at(ctx + 1))

    @pl.when(ctx < count - 1)
    def _():
        halo.start()

    for h in range(halves):
        cols = slice(h * LANES, (h + 1) * LANES)
        for s in range(3):
            pf[s * halves + h, PAD : PAD + tokens, :] = proj[s, :, cols].astype(F32)
        pf[3 * halves + h, PAD : PAD + tokens, :] = cot[:, cols].astype(F32)

    for m in range(modes):
        rate = rates[m : m + 1, :]
        keep = jnp.exp(-rate)
        for h in range(halves):
            lam[h, m] = jnp.broadcast_to(keep[:, h * LANES : (h + 1) * LANES], (SUB, LANES))
            rown[m // quarter, h * quarter + m % quarter : h * quarter + m % quarter + 1, :] = rate[
                :, h * LANES : (h + 1) * LANES
            ]
    steps = lax.broadcasted_iota(jnp.int32, (block, LANES), 0).astype(F32)
    for h in range(halves):
        cols = slice(h * LANES, (h + 1) * LANES)
        total = jnp.zeros((block, LANES), F32)
        for m in range(modes):
            total = total + weights[m : m + 1, cols] * jnp.exp(-rates[m : m + 1, cols] * steps)
        for k in range(block):
            htab[h, k] = jnp.broadcast_to(total[k : k + 1, :], (SUB, LANES))

    def rows(b):
        return pl.ds(PAD + b, SUB, stride=block)

    def tap(s, j, h):
        return jnp.broadcast_to(taps[s, j : j + 1, h * LANES : (h + 1) * LANES], (SUB, LANES))

    def featurize(b, h):
        f = []
        for s in range(3):
            i = s * halves + h
            value = tap(s, 0, h) * pf[i, rows(b), :]
            value = value + tap(s, 1, h) * pf[i, rows(b - 1), :]
            value = value + tap(s, 2, h) * pf[i, rows(b - 2), :]
            feat[i, b] = value
            f.append(value)
        xs[h, b] = f[1] * f[2]
        xs[halves + h, block - 1 - b] = pf[3 * halves + h, rows(b), :] * f[0]

    for h in range(halves):
        lax.fori_loop(2, block, lambda b, _: featurize(b, h), None)

    @pl.when(ctx > 0)
    def _():
        halo.wait_recv()

    for h in range(halves):
        for s in range(3):
            pf[s * halves + h, PAD - 2 : PAD, :] = halo_in[2 * s : 2 * s + 2, h * LANES : (h + 1) * LANES]
        for b in range(2):
            featurize(b, h)

    place = lax.broadcasted_iota(jnp.int32, (SUB, LANES), 0)
    for h in range(halves):
        cols = slice(h * LANES, (h + 1) * LANES)
        keeps = [lam[h, m] for m in range(modes)]

        def horner(b, state):
            front, back = xs[h, b], xs[halves + h, b]
            return tuple(
                state[2 * m + r] * keeps[m] + (front, back)[r] for m in range(modes) for r in range(2)
            )

        zero = jnp.zeros((SUB, LANES), F32)
        state = lax.fori_loop(0, block, horner, (zero,) * (2 * modes))
        for m in range(modes):
            rate = rates[m : m + 1, cols]
            for r in range(2):
                value = state[2 * m + r]
                for k in (1, 2, 4):
                    fade = jnp.exp(-(block * k) * rate)
                    if r == 0:
                        value = value + jnp.where(place >= k, fade, 0.0) * pltpu.roll(value, k, 0)
                    else:
                        value = value + jnp.where(place < SUB - k, fade, 0.0) * pltpu.roll(value, SUB - k, 0)
                row = h * quarter + m % quarter
                owner = r * (G // 2) + m // quarter
                if r == 0:
                    excl[h, m] = jnp.where(place >= 1, pltpu.roll(value, 1, 0), 0.0)
                    sa_out[owner, row : row + 1, :] = value[SUB - 1 : SUB, :]
                else:
                    excl[halves + h, m] = jnp.where(place < SUB - 1, pltpu.roll(value, SUB - 1, 0), 0.0)
                    sa_out[owner, row : row + 1, :] = value[0:1, :]

    group_out = [send(sa_out.at[lax.rem(g + d, G)], sa_in.at[d], S_GROUP, d, at_group(d)) for d in range(1, G)]
    for copy in group_out:
        copy.start()
    sa_in[0] = sa_out[g]

    def direct(hd, _):
        h = lax.rem(hd, halves)
        width = 8
        for b0 in range(0, block, width):
            acc = [None] * width
            for a0 in range(0, b0 + width, width):
                for a in range(a0, a0 + width):
                    x = xs[hd, a]
                    for i in range(width):
                        if b0 + i >= a:
                            term = htab[h, b0 + i - a] * x
                            acc[i] = term if acc[i] is None else acc[i] + term
            for i in range(width):
                ys[hd, b0 + i] = acc[i]

    lax.fori_loop(0, 2, direct, None)
    for copy in group_out:
        copy.wait_recv()

    own_rate = rown[lax.rem(g, G // 2)]
    fade = jnp.exp(-float(tokens) * own_rate)
    fade_group = jnp.exp(-float(tokens * G) * own_rate)

    def member(i):
        return jnp.where(causal, i, G - 1 - i)

    def slot(i):
        return lax.rem(g - member(i) + G, G)

    value = jnp.zeros((SUB, LANES), F32)
    for i in range(G):
        value = value * fade + sa_in[slot(i)]
    sb_out[...] = value
    line_out = [
        send(sb_out, sb_in.at[d], S_LINE, d, at((z + d * towards) * G + g)) for d in range(1, lines)
    ]
    for d in range(1, lines):
        @pl.when(zz + d < lines)
        def _():
            line_out[d - 1].start()

    lax.fori_loop(2, 3, direct, None)
    for d in range(1, lines):
        @pl.when(zz - d >= 0)
        def _():
            line_out[d - 1].wait_recv()

    value = jnp.zeros((SUB, LANES), F32)
    for d in range(lines - 1, 0, -1):
        value = value * fade_group + sb_in[d]
    for i in range(G):
        sc_out[member(i)] = value
        value = value * fade + sa_in[slot(i)]
    back_out = [send(sc_out.at[lax.rem(g + d, G)], sc_in.at[d], S_BACK, d, at_group(d)) for d in range(1, G)]
    for copy in back_out:
        copy.start()
    sc_in[0] = sc_out[g]
    lax.fori_loop(3, 4, direct, None)
    for copy in back_out:
        copy.wait_recv()

    for h in range(halves):
        cols = slice(h * LANES, (h + 1) * LANES)
        keeps = [lam[h, m] for m in range(modes)]
        for r in range(2):
            ahead = (place if r == 0 else SUB - 1 - place).astype(F32)
            left = []
            for m in range(modes):
                owner = r * (G // 2) + m // quarter
                row = h * quarter + m % quarter
                carry = sc_in[lax.rem(g - owner + G, G), row : row + 1, :]
                rate = rates[m : m + 1, cols]
                value = excl[r * halves + h, m] + jnp.exp(-float(block) * rate * ahead) * carry
                left.append(value * (weights[m : m + 1, cols] * keeps[m]))

            def readout(b, left):
                parts = list(left)
                while len(parts) > 1:
                    parts = [parts[i] + parts[i + 1] for i in range(0, len(parts), 2)]
                ys[r * halves + h, b] = ys[r * halves + h, b] + parts[0]
                return tuple(left[m] * keeps[m] for m in range(modes))

            lax.fori_loop(0, block, readout, tuple(left))

    for h in range(halves):
        def finish(b, sums):
            out, back = ys[h, b], ys[halves + h, block - 1 - b]
            gat[h, pl.ds(b, SUB, stride=block), :] = feat[h, b] * out
            fg = (
                pf[3 * halves + h, rows(b), :] * out,
                back * feat[2 * halves + h, b],
                back * feat[halves + h, b],
            )
            result = []
            for s in range(3):
                fgs[s * halves + h, pl.ds(b, SUB, stride=block), :] = fg[s]
                for j in range(3):
                    result.append(sums[3 * s + j] + fg[s] * pf[s * halves + h, rows(b - j), :])
            return tuple(result)

        sums = lax.fori_loop(0, block, finish, (jnp.zeros((SUB, LANES), F32),) * 9)
        for e in range(9):
            unit = e * halves + h
            r1_out[unit // 3, unit % 3 : unit % 3 + 1, :] = jnp.sum(sums[e], axis=0, keepdims=True)
        for s in range(3):
            tail_out[2 * s : 2 * s + 2, h * LANES : (h + 1) * LANES] = fgs[s * halves + h, 0:2, :]

    sum_out = [send(r1_out.at[lax.rem(g + d, G)], r1_in.at[d], R_GROUP, d, at_group(d)) for d in range(1, G)]
    for copy in sum_out:
        copy.start()
    tail = send(tail_out, tail_in, TAIL, 0, at(ctx - 1))

    @pl.when(ctx > 0)
    def _():
        tail.start()

    r1_in[0] = r1_out[g]
    for h in range(halves):
        gated[:, h * LANES : (h + 1) * LANES] = gat[h].astype(gated.dtype)
    for copy in sum_out:
        copy.wait_recv()
    value = r1_in[lax.rem(g + G, G)]
    for i in range(1, G):
        value = value + r1_in[lax.rem(g - i + G, G)]
    r2_out[...] = value
    r2_in[0] = value
    line_sum = [send(r2_out, r2_in.at[d], R_LINE, d, at_line(d)) for d in range(1, lines)]
    for copy in line_sum:
        copy.start()

    @pl.when(ctx < count - 1)
    def _():
        tail.wait_recv()

    for h in range(halves):
        for s in range(3):
            fgs[s * halves + h, tokens : tokens + 2, :] = tail_in[2 * s : 2 * s + 2, h * LANES : (h + 1) * LANES]
    for h in range(halves):
        cols = slice(h * LANES, (h + 1) * LANES)
        for s in range(3):
            i = s * halves + h
            back = taps[s, 0:1, cols] * fgs[i, 0:tokens, :]
            back = back + taps[s, 1:2, cols] * fgs[i, 1 : tokens + 1, :]
            back = back + taps[s, 2:3, cols] * fgs[i, 2 : tokens + 2, :]
            grads[s, :, cols] = back.astype(grads.dtype)

    for copy in line_sum:
        copy.wait_recv()
    value = r2_in[lax.rem(z + lines, lines)]
    for i in range(1, lines):
        value = value + r2_in[lax.rem(z - i + lines, lines)]
    r3_out[...] = value
    r3_in[0] = value
    back_sum = [send(r3_out, r3_in.at[d], R_BACK, d, at_group(d)) for d in range(1, G)]
    for copy in back_sum:
        copy.start()
    for copy in back_sum:
        copy.wait_recv()
    blocks = [r3_in[lax.rem(g - i + G, G)] for i in range(G)]
    square = blocks[0] * blocks[0]
    for i in range(1, G):
        square = square + blocks[i] * blocks[i]
    r4_out[...] = square
    r4_in[0] = square
    norm_out = [send(r4_out, r4_in.at[d], NORM, d, at_tp(d)) for d in range(1, tp_size)]
    for copy in norm_out:
        copy.start()
    for copy in norm_out:
        copy.wait_recv()
    square = r4_in[lax.rem(tp + tp_size, tp_size)]
    for i in range(1, tp_size):
        square = square + r4_in[lax.rem(tp - i + tp_size, tp_size)]
    norm = jnp.sqrt(jnp.sum(jnp.sum(square, axis=0, keepdims=True), axis=1, keepdims=True))
    limit = bound[0]
    scale = limit / jnp.maximum(norm, limit)
    for s in range(3):
        for j in range(3):
            for h in range(halves):
                unit = (3 * s + j) * halves + h
                filt[s, j : j + 1, h * LANES : (h + 1) * LANES] = (
                    blocks[unit // 3][unit % 3 : unit % 3 + 1, :] * scale
                )

    for copy in group_out + back_out + sum_out + line_sum + back_sum + norm_out:
        copy.wait_send()
    for d in range(1, lines):
        @pl.when(zz + d < lines)
        def _():
            line_out[d - 1].wait_send()

    @pl.when(ctx < count - 1)
    def _():
        halo.wait_send()

    @pl.when(ctx > 0)
    def _():
        tail.wait_send()


def local(projected, short_filter, decay_rates, residues, output_grad, clip_bound):
    _, tokens, channels = projected.shape
    modes = decay_rates.shape[0]
    halves = channels // LANES
    block = tokens // SUB
    tp_size = lax.axis_size("tp")
    tile = pltpu.VMEM((SUB, LANES), F32)
    tiles = pltpu.VMEM((G, SUB, LANES), F32)
    edge = pltpu.VMEM((8, channels), F32)
    vmem = pl.BlockSpec(memory_space=pltpu.VMEM)
    return pl.pallas_call(
        functools.partial(kernel, modes, tp_size),
        out_shape=(
            jax.ShapeDtypeStruct((tokens, channels), jnp.bfloat16),
            jax.ShapeDtypeStruct((3, tokens, channels), jnp.bfloat16),
            jax.ShapeDtypeStruct(short_filter.shape, F32),
        ),
        in_specs=[vmem] * 5 + [pl.BlockSpec(memory_space=pltpu.SMEM)],
        out_specs=(vmem, vmem, vmem),
        scratch_shapes=[
            pltpu.VMEM((4 * halves, PAD + tokens, LANES), F32),
            pltpu.VMEM((3 * halves, block, SUB, LANES), F32),
            pltpu.VMEM((2 * halves, block, SUB, LANES), F32),
            pltpu.VMEM((2 * halves, block, SUB, LANES), F32),
            pltpu.VMEM((halves, modes, SUB, LANES), F32),
            pltpu.VMEM((halves, block, SUB, LANES), F32),
            pltpu.VMEM((2 * halves, modes, SUB, LANES), F32),
            pltpu.VMEM((G // 2, SUB, LANES), F32),
            pltpu.VMEM((halves, tokens, LANES), F32),
            pltpu.VMEM((3 * halves, tokens + 8, LANES), F32),
            edge, edge, edge, edge,
            tiles, tiles, tile, tiles, tiles, tiles,
            tiles, tiles, tile, tiles, tile, tiles, tile, tiles,
            pltpu.SemaphoreType.DMA((9, 8)),
            pltpu.SemaphoreType.DMA((9, 8)),
        ],
        compiler_params=pltpu.CompilerParams(
            collective_id=0, has_side_effects=True, vmem_limit_bytes=32 * 1024 * 1024
        ),
    )(projected, short_filter, decay_rates, residues, output_grad, clip_bound)


def solution(mesh):
    placed = (
        P(None, "ctx", "tp"),
        P(None, None, "tp"),
        P(None, "tp"),
        P(None, "tp"),
        P("ctx", "tp"),
        P(),
    )
    return jax.shard_map(
        local,
        mesh=mesh,
        in_specs=placed,
        out_specs=(P("ctx", "tp"), P(None, "ctx", "tp"), P(None, None, "tp")),
        check_vma=False,
    )
```

time: 689 us -> 65.8 us (0.10); the launches traced: 676 us -> 65.4 us
  blocking collectives: 447 us -> 0 us
  local copies, waits for them, and re-layouts: 109 us -> 6.03 us
  Pallas kernels: 0 us -> 58.1 us
  starting transfers between devices: 54.5 us -> 0 us
  waiting for transfers between devices: 29.5 us -> 0 us
  other arithmetic: 27.7 us -> 0 us
    psum x2 -> x0, blocking collectives: 447 us -> none  [the longest x1 408 us: local(): filter_sums = lax.psum(jnp.stack(sums, axis=1), 'ctx')]
    rev x2 -> x0, local copies, waits for them, and re-layouts: 97.8 us -> none  [the longest x1 56.5 us: local(): imag_in = jnp.flip(sliver_grad, 1).reshape(channels, rows, FB)]
    pallas_call x0 -> x1, Pallas kernels: none -> 58.1 us  [local(): pl.pallas_call(functools.partial(kernel, modes, tp_size), out_shape=(jax....]
    all_to_all x4 -> x0, starting transfers between devices: 47.6 us -> none  [the longest x1 15.5 us: local(): lax.all_to_all(jnp.transpose(mixer_input), 'ctx', split_axis=0, concat_ax...]
    all_to_all x4 -> x0, waiting for transfers between devices: 23.3 us -> none  [the longest x1 14.5 us: local(): lax.all_to_all(sliver_back, 'ctx', split_axis=1, concat_axis=0, tiled=True)]
    ppermute x2 -> x0, starting transfers between devices: 6.9 us -> none  [shifted(): lax.ppermute(value, axis, [(source, source + steps) for source in range(l...]
  transfers between devices with their start and end apart: 6 -> 0, of which waited for: 4 -> 0; matrix products, arithmetic and copies ran while one was open for 11% -> 0% of each run, Pallas kernels for 0% -> 0%
where the time goes in v1:
time: 65.8 us; the launch traced here: 65.4 us
  Pallas kernels  58.1 us (88%)
  local copies, waits for them, and re-layouts  6.03 us (9%)
  between operations  1.3 us (2%)
    pallas_call x1, Pallas kernels, local(): pl.pallas_call(functools.partial(kernel, modes, tp_size), out_shape=(jax....  58.1 us
    unnamed x13, local copies, waits for them, and re-layouts  6.03 us

profile of v1, /device:TPU:1, one launch (start us, length us, event | category | flops | bytes accessed | tf_op | source)
XLA Modules:
  0.0 65.4 jit_solution(4057806158964226017)
XLA Ops:
  1.3 0.0 copy-start
  1.3 1.0 %copy-done = bf16[3,256,256]{2,1,0:T(8,128)(2,1)S(1)} copy-done((bf16[3,256,256]{2,1,0:T(8,128)(2,1)S(1)}, bf16[3,256,256]{2,1,0:T(8,128)(2,1)}, u32[]{:S(2)}) %copy-start) | copy-done | bytes 393240
  2.3 0.0 copy-start.1
  2.3 0.9 %copy-done.1 = bf16[256,256]{1,0:T(8,128)(2,1)S(1)} copy-done((bf16[256,256]{1,0:T(8,128)(2,1)S(1)}, bf16[256,256]{1,0:T(8,128)(2,1)}, u32[]{:S(2)}) %copy-start.1) | copy-done | bytes 131096
  3.2 0.0 copy-start.2
  3.2 0.7 %copy-done.2 = f32[16,256]{1,0:T(8,128)S(1)} copy-done((f32[16,256]{1,0:T(8,128)S(1)}, f32[16,256]{1,0:T(8,128)}, u32[]{:S(2)}) %copy-start.2) | copy-done | bytes 16408
  3.9 0.0 copy-start.3
  3.9 0.7 %copy-done.3 = f32[16,256]{1,0:T(8,128)S(1)} copy-done((f32[16,256]{1,0:T(8,128)S(1)}, f32[16,256]{1,0:T(8,128)}, u32[]{:S(2)}) %copy-start.3) | copy-done | bytes 16408
  4.6 0.0 copy-start.4
  4.6 0.7 %copy-done.4 = f32[3,3,256]{2,1,0:T(4,128)S(1)} copy-done((f32[3,3,256]{2,1,0:T(4,128)S(1)}, f32[3,3,256]{2,1,0:T(4,128)}, u32[]{:S(2)}) %copy-start.4) | copy-done | bytes 9240
  5.3 58.1 %shard_map.85 = (bf16[256,256]{1,0:T(8,128)(2,1)S(1)}, bf16[3,256,256]{2,1,0:T(8,128)(2,1)S(1)}, f32[3,3,256]{2,1,0:T(4,128)S(1)}) custom-call(bf16[3,256,256]{2,1,0:T(8,128)(2,1)S(1)} %copy-done, f32[3,3,256]{2,1,0:T(4,128)S(1)} %copy-done.4, f32[16,256]{1,0:T(8,128)S(1)} %copy-done.2, f32[16,256]{1,0:T(8,128)S(1)} %copy-done.3, ...), custom_call_target="tpu_custom_call" | custom-call | tf_op jit(solution)/shard_map/pallas_call | solution.py:398
  63.4 0.7 %copy.13 = bf16[256,256]{1,0:T(8,128)(2,1)} copy(bf16[256,256]{1,0:T(8,128)(2,1)S(1)} %get-tuple-element.6) | data formatting | bytes 262144
  64.1 0.7 %copy.14 = bf16[3,256,256]{2,1,0:T(8,128)(2,1)} copy(bf16[3,256,256]{2,1,0:T(8,128)(2,1)S(1)} %get-tuple-element.7) | data formatting | bytes 786432
  64.8 0.6 copy.15
Async XLA Ops:
  1.3 1.0 %copy-start = (bf16[3,256,256]{2,1,0:T(8,128)(2,1)S(1)}, bf16[3,256,256]{2,1,0:T(8,128)(2,1)}, u32[]{:S(2)}) copy-start(bf16[3,256,256]{2,1,0:T(8,128)(2,1)} %proj.1) | copy-start | bytes 1179652
  2.3 0.9 %copy-start.1 = (bf16[256,256]{1,0:T(8,128)(2,1)S(1)}, bf16[256,256]{1,0:T(8,128)(2,1)}, u32[]{:S(2)}) copy-start(bf16[256,256]{1,0:T(8,128)(2,1)} %cot.1) | copy-start | bytes 393220
  3.2 0.7 %copy-start.2 = (f32[16,256]{1,0:T(8,128)S(1)}, f32[16,256]{1,0:T(8,128)}, u32[]{:S(2)}) copy-start(f32[16,256]{1,0:T(8,128)} %rates.1) | copy-start | bytes 49156
  3.9 0.7 %copy-start.3 = (f32[16,256]{1,0:T(8,128)S(1)}, f32[16,256]{1,0:T(8,128)}, u32[]{:S(2)}) copy-start(f32[16,256]{1,0:T(8,128)} %weights.1) | copy-start | bytes 49156
  4.6 0.7 %copy-start.4 = (f32[3,3,256]{2,1,0:T(4,128)S(1)}, f32[3,3,256]{2,1,0:T(4,128)}, u32[]{:S(2)}) copy-start(f32[3,3,256]{2,1,0:T(4,128)} %taps.1) | copy-start | bytes 27652

commit v2 on v1

v2 whole, which is shorter than its diff:
```python
import functools

import jax
import jax.numpy as jnp
from jax import lax
from jax.experimental import pallas as pl
from jax.experimental.pallas import tpu as pltpu
from jax.sharding import PartitionSpec as P

MESH = pl.DeviceIdType.MESH
F32 = jnp.float32
LANES = 128
SUB = 8
PAD = 8
G = 8
HALO, EDGE, S_GROUP, S_LINE, S_BACK, W_GROUP, R_GROUP, R_RING, R_PLANE, TAIL = range(10)
ROWS = 4
HI = 2


def loop(start, stop, unroll, body, carry):
    def some(i, carry):
        for k in range(unroll):
            carry = body(start + i * unroll + k, carry)
        return carry

    return lax.fori_loop(0, (stop - start) // unroll, some, carry)


def kernel(
    modes, tp_size,
    proj_hbm, taps_hbm, rates_hbm, weights_hbm, cot_hbm, bound,
    gated, grads, filt,
    proj, taps, rates, weights, cot, in_sem,
    pf, feat, xs, ys, lam, htab, excl, rown, wown, gat, fgs,
    halo_out, halo_in, edge_in, tail_out, tail_in,
    sa_out, sa_in, chunk, ga_out, ga_in, sb_out, sb_in, sc_out, sc_in,
    r1_out, r1_in, r2_out, r2_in, r3_out, r3_in,
    ssem, rsem,
):
    loads = [
        pltpu.make_async_copy(src, dst, in_sem.at[i])
        for i, (src, dst) in enumerate(
            ((proj_hbm, proj), (rates_hbm, rates), (taps_hbm, taps), (cot_hbm, cot), (weights_hbm, weights))
        )
    ]
    for load in loads:
        load.start()
    tokens = proj.shape[1]
    halves = proj.shape[2] // LANES
    block = tokens // SUB
    quarter = modes // (G // 2)
    ctx, tp = lax.axis_index("ctx"), lax.axis_index("tp")
    count = lax.axis_size("ctx")
    lines = count // G
    z, g = ctx // G, lax.rem(ctx, G)
    causal = g < G // 2
    zz = jnp.where(causal, z, lines - 1 - z)
    towards = jnp.where(causal, 1, -1)

    def at_group(d):
        return {"ctx": z * G + lax.rem(g + d, G), "tp": tp}

    x, hi = tp // HI, lax.rem(tp, HI)
    ring, planes = HI * lines, tp_size // HI
    zr = hi * lines + z

    def at_ring(d):
        there = lax.rem(zr + d, ring)
        return {"ctx": lax.rem(there, lines) * G + g, "tp": x * HI + there // lines}

    def at_plane(d, e):
        return {"ctx": z * G + lax.rem(g + d, G), "tp": lax.rem(x + e, planes) * HI + hi}

    plane = [(d, e) for e in range(planes) for d in range(G)]

    def at(c):
        return {"ctx": c, "tp": tp}

    halo_in[...] = jnp.zeros_like(halo_in)
    edge_in[...] = jnp.zeros_like(edge_in)
    tail_in[...] = jnp.zeros_like(tail_in)
    sb_in[...] = jnp.zeros_like(sb_in)

    barrier = pltpu.get_barrier_semaphore()
    for d in range(1, ring):
        pl.semaphore_signal(barrier, inc=1, device_id=at_ring(d), device_id_type=MESH)
    for d, e in plane[1:]:
        pl.semaphore_signal(barrier, inc=1, device_id=at_plane(d, e), device_id_type=MESH)
    ends, begins = jnp.logical_and(g == G - 1, z < lines - 1), z > 0

    @pl.when(ends)
    def _():
        for d in range(G - 1):
            pl.semaphore_signal(barrier, inc=1, device_id=at(ctx + 1 + d), device_id_type=MESH)

    @pl.when(jnp.logical_and(begins, g < G - 1))
    def _():
        pl.semaphore_signal(barrier, inc=1, device_id=at(z * G - 1), device_id_type=MESH)

    def send(src, dst, step, d, dev):
        return pltpu.make_async_remote_copy(
            src_ref=src, dst_ref=dst, send_sem=ssem.at[step, d], recv_sem=rsem.at[step, d],
            device_id=dev, device_id_type=MESH,
        )

    tail_out[...] = jnp.zeros_like(tail_out)
    r1_out[...] = jnp.zeros_like(r1_out)
    ga_out[...] = jnp.zeros_like(ga_out)
    halo_out[...] = jnp.zeros_like(halo_out)
    for load in loads:
        load.wait()

    for h in range(halves):
        cols = slice(h * LANES, (h + 1) * LANES)
        for s in range(3):
            pf[s * halves + h, 0:PAD, :] = jnp.zeros((PAD, LANES), F32)
            pf[s * halves + h, PAD : PAD + tokens, :] = proj[s, :, cols].astype(F32)
        pf[3 * halves + h, PAD : PAD + tokens, :] = cot[:, cols].astype(F32)

    for m in range(modes):
        rate = rates[m : m + 1, :]
        keep = jnp.exp(-rate)
        for h in range(halves):
            lam[h, m] = jnp.broadcast_to(keep[:, h * LANES : (h + 1) * LANES], (SUB, LANES))
            row = h * quarter + m % quarter
            rown[m // quarter, row : row + 1, :] = rate[:, h * LANES : (h + 1) * LANES]
            wown[m // quarter, row : row + 1, :] = weights[m : m + 1, h * LANES : (h + 1) * LANES]

    def rows(b):
        return pl.ds(PAD + b, SUB, stride=block)

    def tap(s, j, h):
        return jnp.broadcast_to(taps[s, j : j + 1, h * LANES : (h + 1) * LANES], (SUB, LANES))

    def featurize(b, h):
        f = []
        for s in range(3):
            i = s * halves + h
            value = tap(s, 0, h) * pf[i, rows(b), :]
            value = value + tap(s, 1, h) * pf[i, rows(b - 1), :]
            value = value + tap(s, 2, h) * pf[i, rows(b - 2), :]
            feat[i, b] = value
            f.append(value)
        xs[h, b] = f[1] * f[2]
        xs[halves + h, block - 1 - b] = pf[3 * halves + h, rows(b), :] * f[0]

    place = lax.broadcasted_iota(jnp.int32, (SUB, LANES), 0)
    inner = place >= 1
    for h in range(halves):
        loop(0, block, 4, lambda b, _: featurize(b, h), None)
        for b in range(2):
            xs[h, b] = jnp.where(inner, xs[h, b], 0.0)
            xs[halves + h, block - 1 - b] = jnp.where(inner, xs[halves + h, block - 1 - b], 0.0)

    for h in range(halves):
        cols = slice(h * LANES, (h + 1) * LANES)
        keeps = [lam[h, m] for m in range(modes)]

        def horner(b, state):
            front, back = xs[h, b], xs[halves + h, b]
            return tuple(
                state[2 * m + r] * keeps[m] + (front, back)[r] for m in range(modes) for r in range(2)
            )

        zero = jnp.zeros((SUB, LANES), F32)
        state = loop(0, block, 4, horner, (zero,) * (2 * modes))
        for m in range(modes):
            rate = rates[m : m + 1, cols]
            for r in range(2):
                value = state[2 * m + r]
                for k in (1, 2, 4):
                    fade = jnp.exp(-(block * k) * rate)
                    if r == 0:
                        value = value + jnp.where(place >= k, fade, 0.0) * pltpu.roll(value, k, 0)
                    else:
                        value = value + jnp.where(place < SUB - k, fade, 0.0) * pltpu.roll(value, SUB - k, 0)
                row = h * quarter + m % quarter
                owner = r * (G // 2) + m // quarter
                if r == 0:
                    excl[h, m] = jnp.where(place >= 1, pltpu.roll(value, 1, 0), 0.0)
                    sa_out[owner, row : row + 1, :] = value[SUB - 1 : SUB, :]
                else:
                    excl[halves + h, m] = jnp.where(place < SUB - 1, pltpu.roll(value, SUB - 1, 0), 0.0)
                    sa_out[owner, row : row + 1, :] = value[0:1, :]

    for h in range(halves):
        cols = slice(h * LANES, (h + 1) * LANES)

        def part(s, b):
            i = s * halves + h
            own = [taps[s, j : j + 1, cols] * pf[i, PAD + b - j : PAD + b - j + 1, :] for j in range(b + 1)]
            late = [
                taps[s, j : j + 1, cols] * pf[i, PAD + tokens + b - j : PAD + tokens + b - j + 1, :]
                for j in range(b + 1, 3)
            ]
            return sum(own[1:], own[0]), sum(late[1:], late[0])

        for s in range(3):
            halo_out[2 * s : 2 * s + 2, cols] = pf[s * halves + h, PAD + tokens - 2 : PAD + tokens, :]
        for b in range(2):
            q, k, v = (part(s, b) for s in range(3))
            other = pf[3 * halves + h, PAD + b : PAD + b + 1, :]
            none = jnp.zeros((1, LANES), F32)
            for owner in range(G):
                first, second = (k, v) if owner < G // 2 else ((other, none), q)
                for at_row, kind in ((SUB, 0), (2 * SUB, 1)):
                    row = at_row + b * halves + h
                    sa_out[owner, row : row + 1, :] = first[kind]
                    row = row + 2 * halves
                    sa_out[owner, row : row + 1, :] = second[kind]

    pl.semaphore_wait(
        barrier,
        (ring - 1) + (len(plane) - 1) + jnp.where(ends, G - 1, 0)
        + jnp.where(jnp.logical_and(begins, g < G - 1), 1, 0),
    )
    group_out = [send(sa_out.at[lax.rem(g + d, G)], sa_in.at[d], S_GROUP, d, at_group(d)) for d in range(1, G)]
    for copy in group_out:
        copy.start()
    edges = [
        send(sa_out.at[d, pl.ds(2 * SUB, SUB)], edge_in, EDGE, d, at((z + 1) * G + d)) for d in range(G)
    ]

    @pl.when(ends)
    def _():
        for copy in edges:
            copy.start()

    halo = send(halo_out, halo_in, HALO, 0, at(ctx + 1))

    @pl.when(ctx < count - 1)
    def _():
        halo.start()

    sa_in[0] = sa_out[g]

    chain = modes // 2
    for h in range(halves):
        cols = slice(h * LANES, (h + 1) * LANES)
        for first in range(0, modes, chain):
            keeps = [lam[h, m] for m in range(first, first + chain)]
            for s in range(3):
                def factor(b):
                    return pf[3 * halves + h, rows(b), :] if s == 0 else feat[(3 - s) * halves + h, b]

                def grow(b, state, mask=None):
                    b = block - 1 - b if s == 0 else b
                    with_ = factor(b)
                    if mask is not None:
                        with_ = jnp.where(mask, with_, 0.0)
                    result = []
                    for j in range(3):
                        u = with_ * pf[s * halves + h, rows(b - j), :]
                        result += [state[j * chain + m] * keeps[m] + u for m in range(chain)]
                    return tuple(result)

                state = (jnp.zeros((SUB, LANES), F32),) * (3 * chain)
                if s == 0:
                    state = loop(0, block - 2, 2, grow, state)
                    for b in range(block - 2, block):
                        state = grow(b, state, inner)
                else:
                    for b in range(2):
                        state = grow(b, state, inner)
                    state = loop(2, block, 2, grow, state)
                ahead = (place if s == 0 else SUB - 1 - place).astype(F32)
                for k in range(chain):
                    m = first + k
                    weight = jnp.exp(-(ahead * float(block) + 1.0) * rates[m : m + 1, cols]) * weights[m : m + 1, cols]
                    owner = (0 if s == 0 else G // 2) + m // quarter
                    row = h * quarter + m % quarter
                    for j in range(3):
                        index = j if s == 0 else 3 * (s - 1) + j
                        ga_out[owner, index, row : row + 1, :] = jnp.sum(
                            state[j * chain + k] * weight, axis=0, keepdims=True
                        )

    @pl.when(ctx > 0)
    def _():
        halo.wait_recv()

    for h in range(halves):
        for s in range(3):
            pf[s * halves + h, PAD - 2 : PAD, :] = halo_in[2 * s : 2 * s + 2, h * LANES : (h + 1) * LANES]
        for b in range(2):
            featurize(b, h)

    def both(row_of):
        return jnp.where(place < quarter, row_of(0), row_of(1))

    for q in range(G // 2):
        rate = rown[q]
        weight = wown[q]
        for s in range(3):
            for j in range(3):
                index = j if s == 0 else 3 * (s - 1) + j
                owner = (0 if s == 0 else G // 2) + q
                value = ga_out[owner, index]
                for b in range(2):
                    def product(h):
                        i = s * halves + h
                        if s == 0:
                            with_ = pf[3 * halves + h, PAD + b : PAD + b + 1, :]
                        else:
                            with_ = feat[(3 - s) * halves + h, b, 0:1, :]
                        return with_ * pf[i, PAD + b - j : PAD + b - j + 1, :]

                    power = float(b + 1 if s == 0 else tokens - b)
                    value = value + both(product) * (weight * jnp.exp(-power * rate))
                ga_out[owner, index] = value

    weight_out = [send(ga_out.at[lax.rem(g + d, G)], ga_in.at[d], W_GROUP, d, at_group(d)) for d in range(1, G)]

    for copy in group_out:
        copy.wait_recv()

    @pl.when(begins)
    def _():
        send(sa_out.at[0, pl.ds(2 * SUB, SUB)], edge_in, EDGE, g, at(ctx)).wait_recv()

    own_rate = rown[lax.rem(g, G // 2)]
    fade = jnp.exp(-float(tokens) * own_rate)
    fade_group = jnp.exp(-float(tokens * G) * own_rate)

    def member(i):
        return jnp.where(causal, i, G - 1 - i)

    factors = (
        jnp.where(causal, jnp.exp(-float(tokens - 1) * own_rate), 1.0),
        jnp.where(causal, jnp.exp(-float(tokens - 2) * own_rate), jnp.exp(-own_rate)),
    )
    for i in range(G):
        of = lax.rem(g - i + G, G)
        before = edge_in[...] if i == 0 else sa_in[lax.rem(g - i + 1 + G, G), 2 * SUB : 3 * SUB, :]
        pair = sa_in[of, SUB : 2 * SUB, :] + before
        pair = pair[0 : 2 * halves, :] * pair[2 * halves : 4 * halves, :]
        value = sa_in[of, 0:SUB, :]
        for b in range(2):
            value = value + factors[b] * both(lambda h: pair[b * halves + h : b * halves + h + 1, :])
        chunk[i] = value

    value = jnp.zeros((SUB, LANES), F32)
    for i in range(G):
        value = value * fade + chunk[member(i)]
    sb_out[...] = value
    line_out = [
        send(sb_out, sb_in.at[d], S_LINE, d, at((z + d * towards) * G + g)) for d in range(1, lines)
    ]
    for d in range(1, lines):
        @pl.when(zz + d < lines)
        def _():
            line_out[d - 1].start()

    for copy in weight_out:
        copy.start()
    ga_in[0] = ga_out[g]

    steps = lax.broadcasted_iota(jnp.int32, (block, LANES), 0).astype(F32)
    for h in range(halves):
        cols = slice(h * LANES, (h + 1) * LANES)
        total = jnp.zeros((block, LANES), F32)
        for m in range(modes):
            total = total + weights[m : m + 1, cols] * jnp.exp(-rates[m : m + 1, cols] * steps)
        for k in range(block):
            htab[h, k] = jnp.broadcast_to(total[k : k + 1, :], (SUB, LANES))

    def direct(hd, _):
        h = lax.rem(hd, halves)
        width = 8
        for b0 in range(0, block, width):
            acc = [None] * width
            for a0 in range(0, b0 + width, width):
                for a in range(a0, a0 + width):
                    x = xs[hd, a]
                    for i in range(width):
                        if b0 + i >= a:
                            term = htab[h, b0 + i - a] * x
                            acc[i] = term if acc[i] is None else acc[i] + term
            for i in range(width):
                ys[hd, b0 + i] = acc[i]

    lax.fori_loop(0, 2 * halves, direct, None)

    def readout(h, r, left):
        keeps = [lam[h, m] for m in range(modes)]

        def step(b, left):
            parts = list(left)
            while len(parts) > 1:
                parts = [parts[i] + parts[i + 1] for i in range(0, len(parts), 2)]
            ys[r * halves + h, b] = ys[r * halves + h, b] + parts[0]
            return tuple(left[m] * keeps[m] for m in range(modes))

        loop(0, block, 4, step, tuple(left))

    for h in range(halves):
        cols = slice(h * LANES, (h + 1) * LANES)
        for r in range(2):
            left = []
            for m in range(modes):
                value = excl[r * halves + h, m]
                if r == 0:
                    rate = rates[m : m + 1, cols]
                    behind = jnp.maximum(place - 1, 0).astype(F32) * float(block)
                    late = jnp.exp(-float(block - 1) * rate) * xs[h, 0, 0:1, :]
                    late = late + jnp.exp(-float(block - 2) * rate) * xs[h, 1, 0:1, :]
                    value = value + jnp.where(inner, jnp.exp(-behind * rate) * late, 0.0)
                left.append(value * (weights[m : m + 1, cols] * lam[h, m]))
            readout(h, r, left)

    def feature_grads(b, h):
        out, back = ys[h, b], ys[halves + h, block - 1 - b]
        return out, (
            pf[3 * halves + h, rows(b), :] * out,
            back * feat[2 * halves + h, b],
            back * feat[halves + h, b],
        )

    for h in range(halves):
        def gather(b, sums):
            _, fg = feature_grads(b, h)
            return tuple(
                sums[3 * s + j] + fg[s] * pf[s * halves + h, rows(b - j), :] for s in range(3) for j in range(3)
            )

        sums = loop(0, block, 4, gather, (jnp.zeros((SUB, LANES), F32),) * 9)
        for e in range(9):
            unit = e * halves + h
            r1_out[unit // 3, unit % 3 : unit % 3 + 1, :] = jnp.sum(sums[e], axis=0, keepdims=True)

    for d in range(1, lines):
        @pl.when(zz - d >= 0)
        def _():
            line_out[d - 1].wait_recv()

    value = jnp.zeros((SUB, LANES), F32)
    for d in range(lines - 1, 0, -1):
        value = value * fade_group + sb_in[d]
    for i in range(G):
        sc_out[member(i)] = value
        value = value * fade + chunk[member(i)]
    back_out = [send(sc_out.at[lax.rem(g + d, G)], sc_in.at[d], S_BACK, d, at_group(d)) for d in range(1, G)]
    for copy in back_out:
        copy.start()
    sc_in[0] = sc_out[g]
    for copy in weight_out:
        copy.wait_recv()

    for index in range(6):
        value = jnp.zeros((SUB, LANES), F32)
        for i in range(G):
            value = value + sc_out[i] * ga_in[lax.rem(g - i + G, G), index]
        for h in range(halves):
            total = jnp.sum(value[h * quarter : (h + 1) * quarter, :], axis=0, keepdims=True)
            for here, e in ((causal, index), (jnp.logical_not(causal), index + 3)):
                if e == index and index >= 3:
                    continue
                unit = e * halves + h
                row = unit % 3
                r1_out[unit // 3, row : row + 1, :] = r1_out[unit // 3, row : row + 1, :] + jnp.where(here, total, 0.0)
    sum_out = [send(r1_out.at[lax.rem(g + d, G)], r1_in.at[d], R_GROUP, d, at_group(d)) for d in range(1, G)]
    for copy in sum_out:
        copy.start()
    r1_in[0] = r1_out[g]
    for copy in sum_out:
        copy.wait_recv()
    value = r1_in[lax.rem(g + G, G)]
    for i in range(1, G):
        value = value + r1_in[lax.rem(g - i + G, G)]
    r2_out[...] = value
    r2_in[0] = value
    ring_out = [
        send(r2_out.at[pl.ds(0, ROWS)], r2_in.at[d, pl.ds(0, ROWS)], R_RING, d, at_ring(d)) for d in range(1, ring)
    ]
    for copy in ring_out:
        copy.start()

    for copy in back_out:
        copy.wait_recv()
    for h in range(halves):
        cols = slice(h * LANES, (h + 1) * LANES)
        for r in range(2):
            ahead = (place if r == 0 else SUB - 1 - place).astype(F32)
            left = []
            for m in range(modes):
                owner = r * (G // 2) + m // quarter
                row = h * quarter + m % quarter
                carry = sc_in[lax.rem(g - owner + G, G), row : row + 1, :]
                value = jnp.exp(-(float(block) * ahead + 1.0) * rates[m : m + 1, cols])
                left.append(value * (weights[m : m + 1, cols] * carry))
            readout(h, r, left)

    for h in range(halves):
        def finish(b, _):
            out, fg = feature_grads(b, h)
            gat[h, pl.ds(b, SUB, stride=block), :] = feat[h, b] * out
            for s in range(3):
                fgs[s * halves + h, pl.ds(b, SUB, stride=block), :] = fg[s]

        loop(0, block, 4, finish, None)
        for s in range(3):
            tail_out[2 * s : 2 * s + 2, h * LANES : (h + 1) * LANES] = fgs[s * halves + h, 0:2, :]
    tail = send(tail_out, tail_in, TAIL, 0, at(ctx - 1))

    @pl.when(ctx > 0)
    def _():
        tail.start()

    for h in range(halves):
        gated[:, h * LANES : (h + 1) * LANES] = gat[h].astype(gated.dtype)

    @pl.when(ctx < count - 1)
    def _():
        tail.wait_recv()

    for h in range(halves):
        for s in range(3):
            fgs[s * halves + h, tokens : tokens + 2, :] = tail_in[2 * s : 2 * s + 2, h * LANES : (h + 1) * LANES]
    for h in range(halves):
        cols = slice(h * LANES, (h + 1) * LANES)
        for s in range(3):
            i = s * halves + h
            back = taps[s, 0:1, cols] * fgs[i, 0:tokens, :]
            back = back + taps[s, 1:2, cols] * fgs[i, 1 : tokens + 1, :]
            back = back + taps[s, 2:3, cols] * fgs[i, 2 : tokens + 2, :]
            grads[s, :, cols] = back.astype(grads.dtype)

    for copy in ring_out:
        copy.wait_recv()

    def whole(part):
        value = r2_in[lax.rem(zr - part * lines + ring, ring), 0:ROWS, :]
        for i in range(1, lines):
            value = value + r2_in[lax.rem(zr - part * lines - i + ring, ring), 0:ROWS, :]
        return value

    square = jnp.zeros((1, LANES), F32)
    for part in range(HI):
        value = whole(part)
        square = square + jnp.sum((value * value)[0 : ROWS - 1, :], axis=0, keepdims=True)
    r3_out[...] = whole(hi)
    r3_out[ROWS - 1 : ROWS, :] = square
    r3_in[0] = r3_out[...]
    plane_out = [
        send(r3_out, r3_in.at[i], R_PLANE, i, at_plane(d, e)) for i, (d, e) in enumerate(plane) if i > 0
    ]
    for copy in plane_out:
        copy.start()
    for copy in plane_out:
        copy.wait_recv()

    def from_plane(i, k):
        return r3_in[lax.rem(x - k + planes, planes) * G + lax.rem(g - i + G, G)]

    blocks = [from_plane(i, x) for i in range(G)]
    square = jnp.zeros((1, LANES), F32)
    for k in range(planes):
        for i in range(G):
            square = square + from_plane(i, k)[ROWS - 1 : ROWS, :]
    norm = jnp.sqrt(jnp.sum(square, axis=1, keepdims=True))
    limit = bound[0]
    scale = limit / jnp.maximum(norm, limit)
    for s in range(3):
        for j in range(3):
            for h in range(halves):
                unit = (3 * s + j) * halves + h
                filt[s, j : j + 1, h * LANES : (h + 1) * LANES] = (
                    blocks[unit // 3][unit % 3 : unit % 3 + 1, :] * scale
                )

    for copy in group_out + weight_out + back_out + sum_out + ring_out + plane_out:
        copy.wait_send()
    for d in range(1, lines):
        @pl.when(zz + d < lines)
        def _():
            line_out[d - 1].wait_send()

    @pl.when(ends)
    def _():
        for copy in edges:
            copy.wait_send()

    @pl.when(ctx < count - 1)
    def _():
        halo.wait_send()

    @pl.when(ctx > 0)
    def _():
        tail.wait_send()


def local(projected, short_filter, decay_rates, residues, output_grad, clip_bound):
    _, tokens, channels = projected.shape
    modes = decay_rates.shape[0]
    halves = channels // LANES
    block = tokens // SUB
    tp_size = lax.axis_size("tp")
    lines, planes = lax.axis_size("ctx") // G, tp_size // HI
    tile = pltpu.VMEM((SUB, LANES), F32)
    tiles = pltpu.VMEM((G, SUB, LANES), F32)
    edge = pltpu.VMEM((8, channels), F32)
    vmem = pl.BlockSpec(memory_space=pltpu.VMEM)
    return pl.pallas_call(
        functools.partial(kernel, modes, tp_size),
        out_shape=(
            jax.ShapeDtypeStruct((tokens, channels), jnp.bfloat16),
            jax.ShapeDtypeStruct((3, tokens, channels), jnp.bfloat16),
            jax.ShapeDtypeStruct(short_filter.shape, F32),
        ),
        in_specs=[pl.BlockSpec(memory_space=pltpu.HBM)] * 5 + [pl.BlockSpec(memory_space=pltpu.SMEM)],
        out_specs=(vmem, vmem, vmem),
        scratch_shapes=[
            pltpu.VMEM(projected.shape, projected.dtype),
            pltpu.VMEM(short_filter.shape, F32),
            pltpu.VMEM(decay_rates.shape, F32),
            pltpu.VMEM(residues.shape, F32),
            pltpu.VMEM(output_grad.shape, output_grad.dtype),
            pltpu.SemaphoreType.DMA((5,)),
            pltpu.VMEM((4 * halves, PAD + tokens, LANES), F32),
            pltpu.VMEM((3 * halves, block, SUB, LANES), F32),
            pltpu.VMEM((2 * halves, block, SUB, LANES), F32),
            pltpu.VMEM((2 * halves, block, SUB, LANES), F32),
            pltpu.VMEM((halves, modes, SUB, LANES), F32),
            pltpu.VMEM((halves, block, SUB, LANES), F32),
            pltpu.VMEM((2 * halves, modes, SUB, LANES), F32),
            pltpu.VMEM((G // 2, SUB, LANES), F32),
            pltpu.VMEM((G // 2, SUB, LANES), F32),
            pltpu.VMEM((halves, tokens, LANES), F32),
            pltpu.VMEM((3 * halves, tokens + 8, LANES), F32),
            edge, edge, tile, edge, edge,
            pltpu.VMEM((G, 3 * SUB, LANES), F32), pltpu.VMEM((G, 3 * SUB, LANES), F32), tiles,
            pltpu.VMEM((G, 6, SUB, LANES), F32), pltpu.VMEM((G, 6, SUB, LANES), F32),
            tile, tiles, tiles, tiles,
            tiles, tiles, tile, pltpu.VMEM((HI * lines, SUB, LANES), F32),
            pltpu.VMEM((ROWS, LANES), F32), pltpu.VMEM((G * planes, ROWS, LANES), F32),
            pltpu.SemaphoreType.DMA((10, 32)),
            pltpu.SemaphoreType.DMA((10, 32)),
        ],
        compiler_params=pltpu.CompilerParams(
            collective_id=0, has_side_effects=True, vmem_limit_bytes=32 * 1024 * 1024
        ),
    )(projected, short_filter, decay_rates, residues, output_grad, clip_bound)


def solution(mesh):
    placed = (
        P(None, "ctx", "tp"),
        P(None, None, "tp"),
        P(None, "tp"),
        P(None, "tp"),
        P("ctx", "tp"),
        P(),
    )
    return jax.shard_map(
        local,
        mesh=mesh,
        in_specs=placed,
        out_specs=(P("ctx", "tp"), P(None, "ctx", "tp"), P(None, None, "tp")),
        check_vma=False,
    )
```

time: 65.8 us -> 59.2 us (0.90)
  Pallas kernels: 58.1 us -> 51.5 us
    pallas_call x1, Pallas kernels: 58.1 us -> 51.5 us  [local(): pl.pallas_call(functools.partial(kernel, modes, tp_size), out_shape=(jax....]
where the time goes in v2:
time: 59.2 us; the launch traced here: 58.8 us
  Pallas kernels  51.5 us (87%)
  local copies, waits for them, and re-layouts  6.03 us (10%)
  between operations  1.3 us (2%)
    pallas_call x1, Pallas kernels, local(): pl.pallas_call(functools.partial(kernel, modes, tp_size), out_shape=(jax....  51.5 us
    unnamed x13, local copies, waits for them, and re-layouts  6.03 us

profile of v2, /device:TPU:1, one launch (start us, length us, event | category | flops | bytes accessed | tf_op | source)
XLA Modules:
  0.0 58.8 jit_solution(9418509340910614418)
XLA Ops:
  1.3 0.0 copy-start
  1.3 1.0 %copy-done = bf16[3,256,256]{2,1,0:T(8,128)(2,1)S(1)} copy-done((bf16[3,256,256]{2,1,0:T(8,128)(2,1)S(1)}, bf16[3,256,256]{2,1,0:T(8,128)(2,1)}, u32[]{:S(2)}) %copy-start) | copy-done | bytes 393240
  2.3 0.0 copy-start.1
  2.3 0.9 %copy-done.1 = bf16[256,256]{1,0:T(8,128)(2,1)S(1)} copy-done((bf16[256,256]{1,0:T(8,128)(2,1)S(1)}, bf16[256,256]{1,0:T(8,128)(2,1)}, u32[]{:S(2)}) %copy-start.1) | copy-done | bytes 131096
  3.2 0.0 copy-start.2
  3.2 0.7 %copy-done.2 = f32[16,256]{1,0:T(8,128)S(1)} copy-done((f32[16,256]{1,0:T(8,128)S(1)}, f32[16,256]{1,0:T(8,128)}, u32[]{:S(2)}) %copy-start.2) | copy-done | bytes 16408
  3.9 0.0 copy-start.3
  3.9 0.7 %copy-done.3 = f32[16,256]{1,0:T(8,128)S(1)} copy-done((f32[16,256]{1,0:T(8,128)S(1)}, f32[16,256]{1,0:T(8,128)}, u32[]{:S(2)}) %copy-start.3) | copy-done | bytes 16408
  4.6 0.0 copy-start.4
  4.6 0.7 %copy-done.4 = f32[3,3,256]{2,1,0:T(4,128)S(1)} copy-done((f32[3,3,256]{2,1,0:T(4,128)S(1)}, f32[3,3,256]{2,1,0:T(4,128)}, u32[]{:S(2)}) %copy-start.4) | copy-done | bytes 9240
  5.3 51.5 %shard_map.85 = (bf16[256,256]{1,0:T(8,128)(2,1)S(1)}, bf16[3,256,256]{2,1,0:T(8,128)(2,1)S(1)}, f32[3,3,256]{2,1,0:T(4,128)S(1)}) custom-call(bf16[3,256,256]{2,1,0:T(8,128)(2,1)S(1)} %copy-done, f32[3,3,256]{2,1,0:T(4,128)S(1)} %copy-done.4, f32[16,256]{1,0:T(8,128)S(1)} %copy-done.2, f32[16,256]{1,0:T(8,128)S(1)} %copy-done.3, ...), custom_call_target="tpu_custom_call" | custom-call | tf_op jit(solution)/shard_map/pallas_call | solution.py:604
  56.8 0.7 %copy.13 = bf16[256,256]{1,0:T(8,128)(2,1)} copy(bf16[256,256]{1,0:T(8,128)(2,1)S(1)} %get-tuple-element.6) | data formatting | bytes 262144
  57.5 0.7 %copy.14 = bf16[3,256,256]{2,1,0:T(8,128)(2,1)} copy(bf16[3,256,256]{2,1,0:T(8,128)(2,1)S(1)} %get-tuple-element.7) | data formatting | bytes 786432
  58.2 0.6 %copy.15 = f32[3,3,256]{2,1,0:T(4,128)} copy(f32[3,3,256]{2,1,0:T(4,128)S(1)} %get-tuple-element.8) | data formatting | bytes 18432
Async XLA Ops:
  1.3 1.0 %copy-start = (bf16[3,256,256]{2,1,0:T(8,128)(2,1)S(1)}, bf16[3,256,256]{2,1,0:T(8,128)(2,1)}, u32[]{:S(2)}) copy-start(bf16[3,256,256]{2,1,0:T(8,128)(2,1)} %proj_hbm.1) | copy-start | bytes 1179652
  2.3 0.9 %copy-start.1 = (bf16[256,256]{1,0:T(8,128)(2,1)S(1)}, bf16[256,256]{1,0:T(8,128)(2,1)}, u32[]{:S(2)}) copy-start(bf16[256,256]{1,0:T(8,128)(2,1)} %cot_hbm.1) | copy-start | bytes 393220
  3.2 0.7 %copy-start.2 = (f32[16,256]{1,0:T(8,128)S(1)}, f32[16,256]{1,0:T(8,128)}, u32[]{:S(2)}) copy-start(f32[16,256]{1,0:T(8,128)} %rates_hbm.1) | copy-start | bytes 49156
  3.9 0.7 %copy-start.3 = (f32[16,256]{1,0:T(8,128)S(1)}, f32[16,256]{1,0:T(8,128)}, u32[]{:S(2)}) copy-start(f32[16,256]{1,0:T(8,128)} %weights_hbm.1) | copy-start | bytes 49156
  4.6 0.7 %copy-start.4 = (f32[3,3,256]{2,1,0:T(4,128)S(1)}, f32[3,3,256]{2,1,0:T(4,128)}, u32[]{:S(2)}) copy-start(f32[3,3,256]{2,1,0:T(4,128)} %taps_hbm.1) | copy-start | bytes 27652

commit v3 on v2

--- a/solution.py
+++ b/solution.py
@@ -32,7 +32,7 @@
     proj_hbm, taps_hbm, rates_hbm, weights_hbm, cot_hbm, bound,
     gated, grads, filt,
     proj, taps, rates, weights, cot, in_sem,
-    pf, feat, xs, ys, lam, htab, excl, rown, wown, gat, fgs,
+    pf, ps, feat, xs, ys, lam, htab, excl, rown, wown, gat, fgs,
     halo_out, halo_in, edge_in, tail_out, tail_in,
     sa_out, sa_in, chunk, ga_out, ga_in, sb_out, sb_in, sc_out, sc_in,
     r1_out, r1_in, r2_out, r2_in, r3_out, r3_in,
@@ -137,13 +137,22 @@
         f = []
         for s in range(3):
             i = s * halves + h
-            value = tap(s, 0, h) * pf[i, rows(b), :]
-            value = value + tap(s, 1, h) * pf[i, rows(b - 1), :]
-            value = value + tap(s, 2, h) * pf[i, rows(b - 2), :]
+            value = tap(s, 0, h) * ps[i, b + 2]
+            value = value + tap(s, 1, h) * ps[i, b + 1]
+            value = value + tap(s, 2, h) * ps[i, b]
             feat[i, b] = value
             f.append(value)
         xs[h, b] = f[1] * f[2]
-        xs[halves + h, block - 1 - b] = pf[3 * halves + h, rows(b), :] * f[0]
+        xs[halves + h, block - 1 - b] = ps[3 * halves + h, b + 2] * f[0]
+
+    def turn(i, b):
+        ps[i, b + 2] = pf[i, rows(b), :]
+
+    for i in range(4 * halves):
+        if i < 3 * halves:
+            turn(i, -2)
+            turn(i, -1)
+        loop(0, block, 8, lambda b, _: turn(i, b), None)
 
     place = lax.broadcasted_iota(jnp.int32, (SUB, LANES), 0)
     inner = place >= 1
@@ -210,6 +219,50 @@
                     row = row + 2 * halves
                     sa_out[owner, row : row + 1, :] = second[kind]
 
+    chain = modes // 2
+    def grown(h, first):
+        cols = slice(h * LANES, (h + 1) * LANES)
+        keeps = [lam[h, m] for m in range(first, first + chain)]
+        for s in range(3):
+            def factor(b):
+                return ps[3 * halves + h, b + 2] if s == 0 else feat[(3 - s) * halves + h, b]
+
+            def grow(b, state, mask=None):
+                b = block - 1 - b if s == 0 else b
+                with_ = factor(b)
+                if mask is not None:
+                    with_ = jnp.where(mask, with_, 0.0)
+                result = []
+                for j in range(3):
+                    u = with_ * ps[s * halves + h, b + 2 - j]
+                    result += [state[j * chain + m] * keeps[m] + u for m in range(chain)]
+                return tuple(result)
+
+            state = (jnp.zeros((SUB, LANES), F32),) * (3 * chain)
+            if s == 0:
+                state = loop(0, block - 2, 2, grow, state)
+                for b in range(block - 2, block):
+                    state = grow(b, state, inner)
+            else:
+                for b in range(2):
+                    state = grow(b, state, inner)
+                state = loop(2, block, 2, grow, state)
+            ahead = (place if s == 0 else SUB - 1 - place).astype(F32)
+            for k in range(chain):
+                m = first + k
+                weight = jnp.exp(-(ahead * float(block) + 1.0) * rates[m : m + 1, cols]) * weights[m : m + 1, cols]
+                owner = (0 if s == 0 else G // 2) + m // quarter
+                row = h * quarter + m % quarter
+                for j in range(3):
+                    index = j if s == 0 else 3 * (s - 1) + j
+                    ga_out[owner, index, row : row + 1, :] = jnp.sum(
+                        state[j * chain + k] * weight, axis=0, keepdims=True
+                    )
+
+    pieces = [(h, first) for h in range(halves) for first in range(0, modes, chain)]
+    for piece in pieces[:1]:
+        grown(*piece)
+
     pl.semaphore_wait(
         barrier,
         (ring - 1) + (len(plane) - 1) + jnp.where(ends, G - 1, 0)
@@ -235,82 +288,11 @@
 
     sa_in[0] = sa_out[g]
 
-    chain = modes // 2
-    for h in range(halves):
-        cols = slice(h * LANES, (h + 1) * LANES)
-        for first in range(0, modes, chain):
-            keeps = [lam[h, m] for m in range(first, first + chain)]
-            for s in range(3):
-                def factor(b):
-                    return pf[3 * halves + h, rows(b), :] if s == 0 else feat[(3 - s) * halves + h, b]
-
-                def grow(b, state, mask=None):
-                    b = block - 1 - b if s == 0 else b
-                    with_ = factor(b)
-                    if mask is not None:
-                        with_ = jnp.where(mask, with_, 0.0)
-                    result = []
-                    for j in range(3):
-                        u = with_ * pf[s * halves + h, rows(b - j), :]
-                        result += [state[j * chain + m] * keeps[m] + u for m in range(chain)]
-                    return tuple(result)
-
-                state = (jnp.zeros((SUB, LANES), F32),) * (3 * chain)
-                if s == 0:
-                    state = loop(0, block - 2, 2, grow, state)
-                    for b in range(block - 2, block):
-                        state = grow(b, state, inner)
-                else:
-                    for b in range(2):
-                        state = grow(b, state, inner)
-                    state = loop(2, block, 2, grow, state)
-                ahead = (place if s == 0 else SUB - 1 - place).astype(F32)
-                for k in range(chain):
-                    m = first + k
-                    weight = jnp.exp(-(ahead * float(block) + 1.0) * rates[m : m + 1, cols]) * weights[m : m + 1, cols]
-                    owner = (0 if s == 0 else G // 2) + m // quarter
-                    row = h * quarter + m % quarter
-                    for j in range(3):
-                        index = j if s == 0 else 3 * (s - 1) + j
-                        ga_out[owner, index, row : row + 1, :] = jnp.sum(
-                            state[j * chain + k] * weight, axis=0, keepdims=True
-                        )
-
-    @pl.when(ctx > 0)
-    def _():
-        halo.wait_recv()
-
-    for h in range(halves):
-        for s in range(3):
-            pf[s * halves + h, PAD - 2 : PAD, :] = halo_in[2 * s : 2 * s + 2, h * LANES : (h + 1) * LANES]
-        for b in range(2):
-            featurize(b, h)
+    for piece in pieces[1:4 - 1]:
+        grown(*piece)
 
     def both(row_of):
         return jnp.where(place < quarter, row_of(0), row_of(1))
-
-    for q in range(G // 2):
-        rate = rown[q]
-        weight = wown[q]
-        for s in range(3):
-            for j in range(3):
-                index = j if s == 0 else 3 * (s - 1) + j
-                owner = (0 if s == 0 else G // 2) + q
-                value = ga_out[owner, index]
-                for b in range(2):
-                    def product(h):
-                        i = s * halves + h
-                        if s == 0:
-                            with_ = pf[3 * halves + h, PAD + b : PAD + b + 1, :]
-                        else:
-                            with_ = feat[(3 - s) * halves + h, b, 0:1, :]
-                        return with_ * pf[i, PAD + b - j : PAD + b - j + 1, :]
-
-                    power = float(b + 1 if s == 0 else tokens - b)
-                    value = value + both(product) * (weight * jnp.exp(-power * rate))
-                ga_out[owner, index] = value
-
-    weight_out = [send(ga_out.at[lax.rem(g + d, G)], ga_in.at[d], W_GROUP, d, at_group(d)) for d in range(1, G)]
 
     for copy in group_out:
         copy.wait_recv()
@@ -351,6 +333,44 @@
         @pl.when(zz + d < lines)
         def _():
             line_out[d - 1].start()
+
+    for piece in pieces[4 - 1:]:
+        grown(*piece)
+
+    @pl.when(ctx > 0)
+    def _():
+        halo.wait_recv()
+
+    for h in range(halves):
+        for s in range(3):
+            pf[s * halves + h, PAD - 2 : PAD, :] = halo_in[2 * s : 2 * s + 2, h * LANES : (h + 1) * LANES]
+            turn(s * halves + h, -2)
+            turn(s * halves + h, -1)
+        for b in range(2):
+            featurize(b, h)
+
+    for q in range(G // 2):
+        rate = rown[q]
+        weight = wown[q]
+        for s in range(3):
+            for j in range(3):
+                index = j if s == 0 else 3 * (s - 1) + j
+                owner = (0 if s == 0 else G // 2) + q
+                value = ga_out[owner, index]
+                for b in range(2):
+                    def product(h):
+                        i = s * halves + h
+                        if s == 0:
+                            with_ = pf[3 * halves + h, PAD + b : PAD + b + 1, :]
+                        else:
+                            with_ = feat[(3 - s) * halves + h, b, 0:1, :]
+                        return with_ * pf[i, PAD + b - j : PAD + b - j + 1, :]
+
+                    power = float(b + 1 if s == 0 else tokens - b)
+                    value = value + both(product) * (weight * jnp.exp(-power * rate))
+                ga_out[owner, index] = value
+
+    weight_out = [send(ga_out.at[lax.rem(g + d, G)], ga_in.at[d], W_GROUP, d, at_group(d)) for d in range(1, G)]
 
     for copy in weight_out:
         copy.start()
@@ -412,7 +432,7 @@
     def feature_grads(b, h):
         out, back = ys[h, b], ys[halves + h, block - 1 - b]
         return out, (
-            pf[3 * halves + h, rows(b), :] * out,
+            ps[3 * halves + h, b + 2] * out,
             back * feat[2 * halves + h, b],
             back * feat[halves + h, b],
         )
@@ -421,7 +441,7 @@
         def gather(b, sums):
             _, fg = feature_grads(b, h)
             return tuple(
-                sums[3 * s + j] + fg[s] * pf[s * halves + h, rows(b - j), :] for s in range(3) for j in range(3)
+                sums[3 * s + j] + fg[s] * ps[s * halves + h, b + 2 - j] for s in range(3) for j in range(3)
             )
 
         sums = loop(0, block, 4, gather, (jnp.zeros((SUB, LANES), F32),) * 9)
@@ -618,6 +638,7 @@
             pltpu.VMEM(output_grad.shape, output_grad.dtype),
             pltpu.SemaphoreType.DMA((5,)),
             pltpu.VMEM((4 * halves, PAD + tokens, LANES), F32),
+            pltpu.VMEM((4 * halves, block + 2, SUB, LANES), F32),
             pltpu.VMEM((3 * halves, block, SUB, LANES), F32),
             pltpu.VMEM((2 * halves, block, SUB, LANES), F32),
             pltpu.VMEM((2 * halves, block, SUB, LANES), F32),
@@ -640,7 +661,7 @@
         compiler_params=pltpu.CompilerParams(
             collective_id=0, has_side_effects=True, vmem_limit_bytes=32 * 1024 * 1024
         ),
-    )(projected, short_filter, decay_rates, residues, output_grad, clip_bound)
+    )(*(pltpu.with_memory_space_constraint(v, pltpu.HBM) for v in (projected, short_filter, decay_rates, residues, output_grad)), clip_bound)
 
 
 def solution(mesh):

time: 59.2 us -> 52.3 us (0.88)
  local copies, waits for them, and re-layouts: 6.03 us -> 2 us
  Pallas kernels: 51.5 us -> 48.9 us
    unnamed x13 -> x3, local copies, waits for them, and re-layouts: 6.03 us -> 2 us
    pallas_call x1, Pallas kernels: 51.5 us -> 48.9 us  [local(): pl.pallas_call(functools.partial(kernel, modes, tp_size), out_shape=(jax....]
where the time goes in v3:
time: 52.3 us; the launch traced here: 52.2 us
  Pallas kernels  48.9 us (93%)
  local copies, waits for them, and re-layouts  2 us (4%)
  between operations  1.29 us (2%)
    pallas_call x1, Pallas kernels, local(): pl.pallas_call(functools.partial(kernel, modes, tp_size), out_shape=(jax....  48.9 us
    unnamed x3, local copies, waits for them, and re-layouts  2 us

profile of v3, /device:TPU:1, one launch (start us, length us, event | category | flops | bytes accessed | tf_op | source)
XLA Modules:
  0.0 52.2 jit_solution(7145060162842115946)
XLA Ops:
  1.3 48.9 %shard_map.85 = (bf16[256,256]{1,0:T(8,128)(2,1)S(1)}, bf16[3,256,256]{2,1,0:T(8,128)(2,1)S(1)}, f32[3,3,256]{2,1,0:T(4,128)S(1)}) custom-call(bf16[3,256,256]{2,1,0:T(8,128)(2,1)} %proj_hbm.1, f32[3,3,256]{2,1,0:T(4,128)} %taps_hbm.1, f32[16,256]{1,0:T(8,128)} %rates_hbm.1, f32[16,256]{1,0:T(8,128)} %weights_hbm.1, bf16[256,256]{1,0:T(8,128)(2,1)} %cot_hbm.1, ...), custom_call_target="tpu_custom_call" | custom-call | tf_op jit(solution)/shard_map/pallas_call | solution.py:624
  50.2 0.7 %copy.13 = bf16[256,256]{1,0:T(8,128)(2,1)} copy(bf16[256,256]{1,0:T(8,128)(2,1)S(1)} %get-tuple-element.6) | data formatting | bytes 262144
  50.8 0.7 %copy.14 = bf16[3,256,256]{2,1,0:T(8,128)(2,1)} copy(bf16[3,256,256]{2,1,0:T(8,128)(2,1)S(1)} %get-tuple-element.7) | data formatting | bytes 786432
  51.6 0.6 %copy.15 = f32[3,3,256]{2,1,0:T(4,128)} copy(f32[3,3,256]{2,1,0:T(4,128)S(1)} %get-tuple-element.8) | data formatting | bytes 18432

commit v4 on v3

--- a/solution.py
+++ b/solution.py
@@ -13,7 +13,8 @@
 SUB = 8
 PAD = 8
 G = 8
-HALO, EDGE, S_GROUP, S_LINE, S_BACK, W_GROUP, R_GROUP, R_RING, R_PLANE, TAIL = range(10)
+HALO, EDGE, S_GROUP, S_LINE, S_BACK, W_GROUP, R_GROUP, R_RING, R_PAIR, R_PLANE, TAIL = range(11)
+CORES = 2
 ROWS = 4
 HI = 2
 
@@ -69,10 +70,15 @@
         there = lax.rem(zr + d, ring)
         return {"ctx": lax.rem(there, lines) * G + g, "tp": x * HI + there // lines}
 
-    def at_plane(d, e):
-        return {"ctx": z * G + lax.rem(g + d, G), "tp": lax.rem(x + e, planes) * HI + hi}
-
-    plane = [(d, e) for e in range(planes) for d in range(G)]
+    chips = G // CORES
+    y, core = g // CORES, lax.rem(g, CORES)
+    twin = 1 - core
+
+    def at_plane(i):
+        there = lax.rem(y + lax.rem(i, chips), chips) * CORES + core
+        return {"ctx": z * G + there, "tp": lax.rem(x + i // chips, planes) * HI + hi}
+
+    plane = planes * chips
 
     def at(c):
         return {"ctx": c, "tp": tp}
@@ -83,16 +89,20 @@
     sb_in[...] = jnp.zeros_like(sb_in)
 
     barrier = pltpu.get_barrier_semaphore()
-    for d in range(1, ring):
-        pl.semaphore_signal(barrier, inc=1, device_id=at_ring(d), device_id_type=MESH)
-    for d, e in plane[1:]:
-        pl.semaphore_signal(barrier, inc=1, device_id=at_plane(d, e), device_id_type=MESH)
+    def greet(first, last, dev):
+        def signal(d, _):
+            pl.semaphore_signal(barrier, inc=1, device_id=dev(d), device_id_type=MESH)
+
+        lax.fori_loop(first, last, signal, None)
+
+    greet(1, ring, at_ring)
+    greet(1, G, at_group)
+    greet(chips, plane, at_plane)
     ends, begins = jnp.logical_and(g == G - 1, z < lines - 1), z > 0
 
     @pl.when(ends)
     def _():
-        for d in range(G - 1):
-            pl.semaphore_signal(barrier, inc=1, device_id=at(ctx + 1 + d), device_id_type=MESH)
+        greet(0, G - 1, lambda d: at(ctx + 1 + d))
 
     @pl.when(jnp.logical_and(begins, g < G - 1))
     def _():
@@ -104,6 +114,20 @@
             device_id=dev, device_id_type=MESH,
         )
 
+    def fan(order, src, dst, step, dev):
+        for d in order:
+            send(src(d), dst(d), step, 0, dev(d)).start()
+
+    def far_first(n):
+        return sorted(range(1, n), key=lambda d: -min(d, n - d))
+
+    def through(sems, step, ref):
+        pltpu.make_async_copy(ref, ref, sems.at[step, 0]).wait()
+
+    def member_of(d):
+        return lax.rem(g + d, G)
+
+    rest = pl.ds(1, G - 1)
     tail_out[...] = jnp.zeros_like(tail_out)
     r1_out[...] = jnp.zeros_like(r1_out)
     ga_out[...] = jnp.zeros_like(ga_out)
@@ -265,20 +289,16 @@
 
     pl.semaphore_wait(
         barrier,
-        (ring - 1) + (len(plane) - 1) + jnp.where(ends, G - 1, 0)
+        (ring - 1) + (G - 1) + (plane - chips) + jnp.where(ends, G - 1, 0)
         + jnp.where(jnp.logical_and(begins, g < G - 1), 1, 0),
     )
-    group_out = [send(sa_out.at[lax.rem(g + d, G)], sa_in.at[d], S_GROUP, d, at_group(d)) for d in range(1, G)]
-    for copy in group_out:
-        copy.start()
-    edges = [
-        send(sa_out.at[d, pl.ds(2 * SUB, SUB)], edge_in, EDGE, d, at((z + 1) * G + d)) for d in range(G)
-    ]
-
+    fan(far_first(G), lambda d: sa_out.at[member_of(d)], lambda d: sa_in.at[d], S_GROUP, at_group)
     @pl.when(ends)
     def _():
-        for copy in edges:
-            copy.start()
+        fan(
+            range(G), lambda d: sa_out.at[d, pl.ds(2 * SUB, SUB)], lambda d: edge_in, EDGE,
+            lambda d: at((z + 1) * G + d),
+        )
 
     halo = send(halo_out, halo_in, HALO, 0, at(ctx + 1))
 
@@ -294,12 +314,11 @@
     def both(row_of):
         return jnp.where(place < quarter, row_of(0), row_of(1))
 
-    for copy in group_out:
-        copy.wait_recv()
+    through(rsem, S_GROUP, sa_in.at[rest])
 
     @pl.when(begins)
     def _():
-        send(sa_out.at[0, pl.ds(2 * SUB, SUB)], edge_in, EDGE, g, at(ctx)).wait_recv()
+        through(rsem, EDGE, edge_in)
 
     own_rate = rown[lax.rem(g, G // 2)]
     fade = jnp.exp(-float(tokens) * own_rate)
@@ -326,14 +345,13 @@
     for i in range(G):
         value = value * fade + chunk[member(i)]
     sb_out[...] = value
-    line_out = [
-        send(sb_out, sb_in.at[d], S_LINE, d, at((z + d * towards) * G + g)) for d in range(1, lines)
-    ]
-    for d in range(1, lines):
-        @pl.when(zz + d < lines)
-        def _():
-            line_out[d - 1].start()
-
+    def along(d):
+        return send(sb_out, sb_in.at[d], S_LINE, d, at((z + d * towards) * G + g))
+
+    def line_loop(last, act):
+        lax.fori_loop(1, last, lambda d, _: act(along(last - d)), None)
+
+    line_loop(lines - zz, lambda copy: copy.start())
     for piece in pieces[4 - 1:]:
         grown(*piece)
 
@@ -370,10 +388,8 @@
                     value = value + both(product) * (weight * jnp.exp(-power * rate))
                 ga_out[owner, index] = value
 
-    weight_out = [send(ga_out.at[lax.rem(g + d, G)], ga_in.at[d], W_GROUP, d, at_group(d)) for d in range(1, G)]
-
-    for copy in weight_out:
-        copy.start()
+
+    fan(far_first(G), lambda d: ga_out.at[member_of(d)], lambda d: ga_in.at[d], W_GROUP, at_group)
     ga_in[0] = ga_out[g]
 
     steps = lax.broadcasted_iota(jnp.int32, (block, LANES), 0).astype(F32)
@@ -449,23 +465,16 @@
             unit = e * halves + h
             r1_out[unit // 3, unit % 3 : unit % 3 + 1, :] = jnp.sum(sums[e], axis=0, keepdims=True)
 
-    for d in range(1, lines):
-        @pl.when(zz - d >= 0)
-        def _():
-            line_out[d - 1].wait_recv()
-
+    line_loop(zz + 1, lambda copy: copy.wait_recv())
     value = jnp.zeros((SUB, LANES), F32)
     for d in range(lines - 1, 0, -1):
         value = value * fade_group + sb_in[d]
     for i in range(G):
         sc_out[member(i)] = value
         value = value * fade + chunk[member(i)]
-    back_out = [send(sc_out.at[lax.rem(g + d, G)], sc_in.at[d], S_BACK, d, at_group(d)) for d in range(1, G)]
-    for copy in back_out:
-        copy.start()
+    fan(far_first(G), lambda d: sc_out.at[member_of(d)], lambda d: sc_in.at[d], S_BACK, at_group)
     sc_in[0] = sc_out[g]
-    for copy in weight_out:
-        copy.wait_recv()
+    through(rsem, W_GROUP, ga_in.at[rest])
 
     for index in range(6):
         value = jnp.zeros((SUB, LANES), F32)
@@ -479,25 +488,17 @@
                 unit = e * halves + h
                 row = unit % 3
                 r1_out[unit // 3, row : row + 1, :] = r1_out[unit // 3, row : row + 1, :] + jnp.where(here, total, 0.0)
-    sum_out = [send(r1_out.at[lax.rem(g + d, G)], r1_in.at[d], R_GROUP, d, at_group(d)) for d in range(1, G)]
-    for copy in sum_out:
-        copy.start()
+    fan(far_first(G), lambda d: r1_out.at[member_of(d)], lambda d: r1_in.at[d], R_GROUP, at_group)
     r1_in[0] = r1_out[g]
-    for copy in sum_out:
-        copy.wait_recv()
+    through(rsem, R_GROUP, r1_in.at[rest])
     value = r1_in[lax.rem(g + G, G)]
     for i in range(1, G):
         value = value + r1_in[lax.rem(g - i + G, G)]
-    r2_out[...] = value
-    r2_in[0] = value
-    ring_out = [
-        send(r2_out.at[pl.ds(0, ROWS)], r2_in.at[d, pl.ds(0, ROWS)], R_RING, d, at_ring(d)) for d in range(1, ring)
-    ]
-    for copy in ring_out:
-        copy.start()
-
-    for copy in back_out:
-        copy.wait_recv()
+    r2_out[...] = value[0:ROWS, :]
+    r2_in[0] = value[0:ROWS, :]
+    fan(far_first(ring), lambda d: r2_out, lambda d: r2_in.at[d], R_RING, at_ring)
+
+    through(rsem, S_BACK, sc_in.at[rest])
     for h in range(halves):
         cols = slice(h * LANES, (h + 1) * LANES)
         for r in range(2):
@@ -546,38 +547,47 @@
             back = back + taps[s, 2:3, cols] * fgs[i, 2 : tokens + 2, :]
             grads[s, :, cols] = back.astype(grads.dtype)
 
-    for copy in ring_out:
-        copy.wait_recv()
+    through(rsem, R_RING, r2_in.at[pl.ds(1, ring - 1)])
 
     def whole(part):
-        value = r2_in[lax.rem(zr - part * lines + ring, ring), 0:ROWS, :]
+        value = r2_in[lax.rem(zr - part * lines + ring, ring)]
         for i in range(1, lines):
-            value = value + r2_in[lax.rem(zr - part * lines - i + ring, ring), 0:ROWS, :]
+            value = value + r2_in[lax.rem(zr - part * lines - i + ring, ring)]
         return value
 
     square = jnp.zeros((1, LANES), F32)
     for part in range(HI):
         value = whole(part)
         square = square + jnp.sum((value * value)[0 : ROWS - 1, :], axis=0, keepdims=True)
-    r3_out[...] = whole(hi)
-    r3_out[ROWS - 1 : ROWS, :] = square
+    for c in range(CORES):
+        @pl.when(core == c)
+        def _():
+            r3_out[c * ROWS : (c + 1) * ROWS, :] = whole(hi)
+            r3_out[(c + 1) * ROWS - 1 : (c + 1) * ROWS, :] = square
+
+    pair = send(
+        r3_out.at[pl.ds(core * ROWS, ROWS)], r3_out.at[pl.ds(core * ROWS, ROWS)], R_PAIR, 0, at(z * G + y * CORES + twin)
+    )
+    pair.start()
+    through(rsem, R_PAIR, r3_out.at[pl.ds(twin * ROWS, ROWS)])
     r3_in[0] = r3_out[...]
-    plane_out = [
-        send(r3_out, r3_in.at[i], R_PLANE, i, at_plane(d, e)) for i, (d, e) in enumerate(plane) if i > 0
-    ]
-    for copy in plane_out:
-        copy.start()
-    for copy in plane_out:
-        copy.wait_recv()
+    across = sorted(
+        range(1, plane), key=lambda i: -(min(i % chips, chips - i % chips) + min(i // chips, planes - i // chips))
+    )
+    fan(across, lambda i: r3_out, lambda i: r3_in.at[i], R_PLANE, at_plane)
+    through(rsem, R_PLANE, r3_in.at[pl.ds(1, plane - 1)])
 
     def from_plane(i, k):
-        return r3_in[lax.rem(x - k + planes, planes) * G + lax.rem(g - i + G, G)]
-
-    blocks = [from_plane(i, x) for i in range(G)]
+        return r3_in[lax.rem(x - k + planes, planes) * chips + lax.rem(y - i + chips, chips)]
+
+    pairs = [from_plane(i, x) for i in range(chips)]
+    blocks = [pairs[i // CORES][i % CORES * ROWS : (i % CORES + 1) * ROWS, :] for i in range(G)]
     square = jnp.zeros((1, LANES), F32)
     for k in range(planes):
-        for i in range(G):
-            square = square + from_plane(i, k)[ROWS - 1 : ROWS, :]
+        for i in range(chips):
+            both_cores = from_plane(i, k)
+            for c in range(CORES):
+                square = square + both_cores[(c + 1) * ROWS - 1 : (c + 1) * ROWS, :]
     norm = jnp.sqrt(jnp.sum(square, axis=1, keepdims=True))
     limit = bound[0]
     scale = limit / jnp.maximum(norm, limit)
@@ -589,17 +599,18 @@
                     blocks[unit // 3][unit % 3 : unit % 3 + 1, :] * scale
                 )
 
-    for copy in group_out + weight_out + back_out + sum_out + ring_out + plane_out:
-        copy.wait_send()
-    for d in range(1, lines):
-        @pl.when(zz + d < lines)
-        def _():
-            line_out[d - 1].wait_send()
+    for step, ref in (
+        (S_GROUP, sa_in), (W_GROUP, ga_in), (S_BACK, sc_in), (R_GROUP, r1_in),
+    ):
+        through(ssem, step, ref.at[rest])
+    through(ssem, R_RING, r2_in.at[pl.ds(1, ring - 1)])
+    pair.wait_send()
+    through(ssem, R_PLANE, r3_in.at[pl.ds(1, plane - 1)])
+    line_loop(lines - zz, lambda copy: copy.wait_send())
 
     @pl.when(ends)
     def _():
-        for copy in edges:
-            copy.wait_send()
+        through(ssem, EDGE, sa_out.at[pl.ds(0, G), pl.ds(2 * SUB, SUB)])
 
     @pl.when(ctx < count - 1)
     def _():
@@ -653,10 +664,10 @@
             pltpu.VMEM((G, 3 * SUB, LANES), F32), pltpu.VMEM((G, 3 * SUB, LANES), F32), tiles,
             pltpu.VMEM((G, 6, SUB, LANES), F32), pltpu.VMEM((G, 6, SUB, LANES), F32),
             tile, tiles, tiles, tiles,
-            tiles, tiles, tile, pltpu.VMEM((HI * lines, SUB, LANES), F32),
-            pltpu.VMEM((ROWS, LANES), F32), pltpu.VMEM((G * planes, ROWS, LANES), F32),
-            pltpu.SemaphoreType.DMA((10, 32)),
-            pltpu.SemaphoreType.DMA((10, 32)),
+            tiles, tiles, pltpu.VMEM((ROWS, LANES), F32), pltpu.VMEM((HI * lines, ROWS, LANES), F32),
+            pltpu.VMEM((CORES * ROWS, LANES), F32), pltpu.VMEM((G // CORES * planes, CORES * ROWS, LANES), F32),
+            pltpu.SemaphoreType.DMA((11, 8)),
+            pltpu.SemaphoreType.DMA((11, 8)),
         ],
         compiler_params=pltpu.CompilerParams(
             collective_id=0, has_side_effects=True, vmem_limit_bytes=32 * 1024 * 1024

time: 52.3 us -> 47.5 us (0.908)
  Pallas kernels: 48.9 us -> 44.1 us
    pallas_call x1, Pallas kernels: 48.9 us -> 44.1 us  [local(): pl.pallas_call(functools.partial(kernel, modes, tp_size), out_shape=(jax....]
where the time goes in v4:
time: 47.5 us; the launch traced here: 47.4 us
  Pallas kernels  44.1 us (93%)
  local copies, waits for them, and re-layouts  2 us (4%)
  between operations  1.29 us (3%)
    pallas_call x1, Pallas kernels, local(): pl.pallas_call(functools.partial(kernel, modes, tp_size), out_shape=(jax....  44.1 us
    unnamed x3, local copies, waits for them, and re-layouts  2 us

profile of v4, /device:TPU:1, one launch (start us, length us, event | category | flops | bytes accessed | tf_op | source)
XLA Modules:
  0.0 47.4 jit_solution(9302716233754696478)
XLA Ops:
  1.3 44.1 %shard_map.85 = (bf16[256,256]{1,0:T(8,128)(2,1)S(1)}, bf16[3,256,256]{2,1,0:T(8,128)(2,1)S(1)}, f32[3,3,256]{2,1,0:T(4,128)S(1)}) custom-call(bf16[3,256,256]{2,1,0:T(8,128)(2,1)} %proj_hbm.1, f32[3,3,256]{2,1,0:T(4,128)} %taps_hbm.1, f32[16,256]{1,0:T(8,128)} %rates_hbm.1, f32[16,256]{1,0:T(8,128)} %weights_hbm.1, bf16[256,256]{1,0:T(8,128)(2,1)} %cot_hbm.1, ...), custom_call_target="tpu_custom_call" | custom-call | tf_op jit(solution)/shard_map/pallas_call | solution.py:635
  45.4 0.7 %copy.13 = bf16[256,256]{1,0:T(8,128)(2,1)} copy(bf16[256,256]{1,0:T(8,128)(2,1)S(1)} %get-tuple-element.6) | data formatting | bytes 262144
  46.1 0.7 %copy.14 = bf16[3,256,256]{2,1,0:T(8,128)(2,1)} copy(bf16[3,256,256]{2,1,0:T(8,128)(2,1)S(1)} %get-tuple-element.7) | data formatting | bytes 786432
  46.8 0.6 %copy.15 = f32[3,3,256]{2,1,0:T(4,128)} copy(f32[3,3,256]{2,1,0:T(4,128)S(1)} %get-tuple-element.8) | data formatting | bytes 18432

commit v5 on v4

--- a/solution.py
+++ b/solution.py
@@ -472,8 +472,6 @@
     for i in range(G):
         sc_out[member(i)] = value
         value = value * fade + chunk[member(i)]
-    fan(far_first(G), lambda d: sc_out.at[member_of(d)], lambda d: sc_in.at[d], S_BACK, at_group)
-    sc_in[0] = sc_out[g]
     through(rsem, W_GROUP, ga_in.at[rest])
 
     for index in range(6):
@@ -489,6 +487,8 @@
                 row = unit % 3
                 r1_out[unit // 3, row : row + 1, :] = r1_out[unit // 3, row : row + 1, :] + jnp.where(here, total, 0.0)
     fan(far_first(G), lambda d: r1_out.at[member_of(d)], lambda d: r1_in.at[d], R_GROUP, at_group)
+    fan(far_first(G), lambda d: sc_out.at[member_of(d)], lambda d: sc_in.at[d], S_BACK, at_group)
+    sc_in[0] = sc_out[g]
     r1_in[0] = r1_out[g]
     through(rsem, R_GROUP, r1_in.at[rest])
     value = r1_in[lax.rem(g + G, G)]
@@ -664,7 +664,8 @@
             pltpu.VMEM((G, 3 * SUB, LANES), F32), pltpu.VMEM((G, 3 * SUB, LANES), F32), tiles,
             pltpu.VMEM((G, 6, SUB, LANES), F32), pltpu.VMEM((G, 6, SUB, LANES), F32),
             tile, tiles, tiles, tiles,
-            tiles, tiles, pltpu.VMEM((ROWS, LANES), F32), pltpu.VMEM((HI * lines, ROWS, LANES), F32),
+            pltpu.VMEM((G, ROWS, LANES), F32), pltpu.VMEM((G, ROWS, LANES), F32),
+            pltpu.VMEM((ROWS, LANES), F32), pltpu.VMEM((HI * lines, ROWS, LANES), F32),
             pltpu.VMEM((CORES * ROWS, LANES), F32), pltpu.VMEM((G // CORES * planes, CORES * ROWS, LANES), F32),
             pltpu.SemaphoreType.DMA((11, 8)),
             pltpu.SemaphoreType.DMA((11, 8)),

time: 47.5 us -> 47.3 us (level)
  no operation moved by 1% of the time
where the time goes in v5:
time: 47.3 us; the launch traced here: 47.2 us
  Pallas kernels  43.9 us (93%)
  local copies, waits for them, and re-layouts  2 us (4%)
  between operations  1.29 us (3%)
    pallas_call x1, Pallas kernels, local(): pl.pallas_call(functools.partial(kernel, modes, tp_size), out_shape=(jax....  43.9 us
    unnamed x3, local copies, waits for them, and re-layouts  2 us

profile of v5, /device:TPU:1, one launch (start us, length us, event | category | flops | bytes accessed | tf_op | source)
XLA Modules:
  0.0 47.2 jit_solution(3778338983726322790)
XLA Ops:
  1.3 43.9 %shard_map.85 = (bf16[256,256]{1,0:T(8,128)(2,1)S(1)}, bf16[3,256,256]{2,1,0:T(8,128)(2,1)S(1)}, f32[3,3,256]{2,1,0:T(4,128)S(1)}) custom-call(bf16[3,256,256]{2,1,0:T(8,128)(2,1)} %proj_hbm.1, f32[3,3,256]{2,1,0:T(4,128)} %taps_hbm.1, f32[16,256]{1,0:T(8,128)} %rates_hbm.1, f32[16,256]{1,0:T(8,128)} %weights_hbm.1, bf16[256,256]{1,0:T(8,128)(2,1)} %cot_hbm.1, ...), custom_call_target="tpu_custom_call" | custom-call | tf_op jit(solution)/shard_map/pallas_call | solution.py:635
  45.2 0.7 %copy.13 = bf16[256,256]{1,0:T(8,128)(2,1)} copy(bf16[256,256]{1,0:T(8,128)(2,1)S(1)} %get-tuple-element.6) | data formatting | bytes 262144
  45.8 0.7 %copy.14 = bf16[3,256,256]{2,1,0:T(8,128)(2,1)} copy(bf16[3,256,256]{2,1,0:T(8,128)(2,1)S(1)} %get-tuple-element.7) | data formatting | bytes 786432
  46.6 0.6 %copy.15 = f32[3,3,256]{2,1,0:T(4,128)} copy(f32[3,3,256]{2,1,0:T(4,128)S(1)} %get-tuple-element.8) | data formatting | bytes 18432
